TPU v7x, 256 devices: a whole 4x4x8 slice. The times are simulated.
256 devices in a mesh: dp: 32 (over y, x, core), mp: 8 (over z).
Axes of the slice: x: 4, y: 4, z: 8, core: 2. Of those that a mesh axis runs over, the one named last changes fastest.
Arguments:
- tokens_in: bfloat16 [24576, 2048], P(('dp', 'mp')), may hold values from -6 to 6
- pre_act: bfloat16 [24576, 12288], P('dp', 'mp'), may hold values from -8 to 8
- grad_hidden: bfloat16 [24576, 12288], P('dp', 'mp'), may hold values from -0.0625 to 0.0625
- sample_tokens: int32 [32, 3], P('dp'), may hold values from 1 to 256, 672 in all within a row
- block_slot: int32 [8, 12], P('mp'), may hold values from 0 to 31, as said below
- moment: bfloat16 [8, 32, 512, 512], P('mp', 'dp'), may hold values from -0.59765625 to 0.59765625
- second: bfloat16 [8, 32, 512, 512], P('mp', 'dp'), may hold values from 0.019897461 to 0.19921875
- left: float32 [8, 32, 512, 512], P('mp', 'dp'), may hold values from -6 to 6
- right: float32 [8, 32, 512, 512], P('mp', 'dp'), may hold values from -6 to 6
- basis_left: bfloat16 [8, 32, 512, 512], P('mp', 'dp'), as said below
- basis_right: bfloat16 [8, 32, 512, 512], P('mp', 'dp'), as said below
Outputs:
- direction: bfloat16 [2048, 12288], P('dp', 'mp')
- moment_out: bfloat16 [8, 32, 512, 512], P('mp', 'dp')
- second_out: bfloat16 [8, 32, 512, 512], P('mp', 'dp')
- left_out: float32 [8, 32, 512, 512], P('mp', 'dp')
- right_out: float32 [8, 32, 512, 512], P('mp', 'dp')
Inputs may be any that keep to these rules, and one draw needn't show every extreme that they name: `block_slot`: slot s belongs to data-group index s. Within each row the entries are distinct, so an owner holds at most 1 block of a hidden-unit shard, and in every row some owner holds exactly 1. Every row lists slot 0 and slot 31. `basis_left`: each [512, 512] matrix is orthogonal up to bfloat16 rounding. `basis_right`: each [512, 512] matrix is orthogonal up to bfloat16 rounding. `sample_tokens`: the counts of each data group sum to 672, and the largest is 256.
All inputs are finite; a program needn't handle non-finite values.
Results may differ from a plain program's by a relative error of at most 0.03.
Values may be sent and summed in bfloat16 or wider, within the bound.
No kernel may reach another device: no remote copies, remote signals or barrier semaphores. Data moves between devices by JAX's collectives and lax.ppermute only.
A program may use at most 128 MiB of HBM per device.

v0:
```python
import functools

import jax
import jax.numpy as jnp
from jax import lax
from jax.experimental import pallas as pl
from jax.experimental.pallas import tpu as pltpu
from jax.sharding import PartitionSpec as P

SEQ = 256
X_CHIPS = 4
Y_CHIPS = 4
CORES = 2
Z_CHIPS = 8
STRIP = 16

momentum_decay = 0.9
factor_decay = 0.95
adam_epsilon = 1e-08

FRONT = (((0,), (0,)), ((), ()))
BACK = (((1,), (1,)), ((), ()))
VMEM_LIMIT = 24 * 1024 * 1024


def params(*semantics):
    return pltpu.CompilerParams(
        dimension_semantics=semantics or None, vmem_limit_bytes=VMEM_LIMIT
    )


def core_swap():
    return [(i, i ^ 1) for i in range(32)]


def x_swap(k):
    return [(i, i ^ (CORES * k)) for i in range(32)]


def y_swap(k):
    return [(i, i ^ (CORES * X_CHIPS * k)) for i in range(32)]


def z_swap(odd):
    pairs = [(i, (i + 1) % Z_CHIPS) for i in range(odd, Z_CHIPS, 2)]
    return pairs + [(j, i) for i, j in pairs]


def gelu_slope(values):
    cumulative = 0.5 * (1.0 + lax.erf(values * 0.7071067811865476))
    density = jnp.exp(-0.5 * values * values) * 0.3989422804014327
    return cumulative + values * density


def pre_grad_kernel(info, pre_ref, grad_ref, out_ref):
    shard_rows, width = pre_ref.shape
    shard = info[pl.program_id(0)]
    position = shard * shard_rows + lax.broadcasted_iota(jnp.int32, (shard_rows, width), 0)
    member = position // SEQ
    limits = jnp.where(member == 0, info[8], jnp.where(member == 1, info[9], info[10]))
    keep = position - member * SEQ < limits
    slope = gelu_slope(pre_ref[...].astype(jnp.float32))
    out_ref[...] = jnp.where(keep, grad_ref[...].astype(jnp.float32) * slope, 0.0).astype(
        out_ref.dtype
    )


def make_pre_grad(pre_act, grad_hidden, info):
    rows, width = pre_act.shape
    shard_rows = rows // Z_CHIPS
    rolled = pl.BlockSpec((shard_rows, width), lambda d, info: (info[d], 0))
    return pl.pallas_call(
        pre_grad_kernel,
        grid_spec=pltpu.PrefetchScalarGridSpec(
            num_scalar_prefetch=1,
            grid=(Z_CHIPS,),
            in_specs=[rolled, rolled],
            out_specs=pl.BlockSpec((shard_rows, width), lambda d, info: (d, 0)),
        ),
        out_shape=jax.ShapeDtypeStruct((rows, width), jnp.bfloat16),
        compiler_params=params("arbitrary"),
        cost_estimate=pl.CostEstimate(
            flops=40 * rows * width, bytes_accessed=6 * rows * width, transcendentals=rows * width
        ),
        name="pre_grad",
    )(info, pre_act, grad_hidden)


def stack_rows(shards, rows):
    for place, shard in enumerate(shards):
        count = shard.shape[0]
        rows[pl.ds(place * count, count), :] = shard[...]


def product_rows(rows, grads, first, m, tile):
    left = pl.ds(pl.multiple_of(m * tile, tile), tile)
    return lax.dot_general(
        rows[:, left],
        grads[pl.ds(first, rows.shape[0]), :],
        FRONT,
        preferred_element_type=jnp.float32,
    )


def gather_kernel(count_own, count_sib, first_own, first_sib, resume, *refs):
    own, sib, refs = refs[:count_own], refs[count_own : count_own + count_sib], refs[count_own + count_sib :]
    grads_own, grads_sib = refs[:2]
    before = refs[2] if resume else None
    total, rows_own, rows_sib, held_sib, sem = refs[-5:]
    depth = held_sib.shape[0]
    copy = pltpu.make_async_copy(grads_sib.at[pl.ds(first_sib, depth), :], held_sib, sem)
    copy.start()
    tile = 512
    if own:
        stack_rows(own, rows_own)
    stack_rows(sib, rows_sib)
    copy.wait()

    def step(m, carry):
        product = product_rows(rows_sib, held_sib, 0, m, tile)
        if own:
            product += product_rows(rows_own, grads_own, first_own, m, tile)
        here = pl.ds(pl.multiple_of(m * tile, tile), tile)
        if resume:
            product += before[here, :].astype(jnp.float32)
        total[here, :] = product.astype(total.dtype)
        return carry

    lax.fori_loop(0, total.shape[0] // tile, step, 0)


def make_gathered(own, sib, grads_own, grads_sib, first_own, first_sib, before=None):
    width = grads_own.shape[1]
    rows, chunk = sib[0].shape
    depth_own, depth_sib = max(len(own), 1) * rows, len(sib) * rows
    vmem = pl.BlockSpec(memory_space=pltpu.VMEM)
    operands = [*own, *sib, grads_own, grads_sib] + ([] if before is None else [before])
    specs = [vmem] * len(operands)
    specs[len(own) + len(sib) + 1] = pl.BlockSpec(memory_space=pl.ANY)
    return pl.pallas_call(
        functools.partial(
            gather_kernel, len(own), len(sib), first_own * rows, first_sib * rows, before is not None
        ),
        in_specs=specs,
        out_specs=vmem,
        out_shape=jax.ShapeDtypeStruct((chunk, width), jnp.bfloat16),
        scratch_shapes=[
            pltpu.VMEM((depth_own, chunk), jnp.bfloat16),
            pltpu.VMEM((depth_sib, chunk), jnp.bfloat16),
            pltpu.VMEM((depth_sib, width), jnp.bfloat16),
            pltpu.SemaphoreType.DMA,
        ],
        input_output_aliases={} if before is None else {len(operands) - 1: 0},
        compiler_params=params(),
        cost_estimate=pl.CostEstimate(
            flops=2 * (len(own) * rows + depth_sib) * width * chunk,
            bytes_accessed=4 * width * chunk,
            transcendentals=0,
        ),
        name="gathered",
    )(*operands)


def partial_kernel(x_first, first, info, *refs):
    rows_own, rows_sib, grads_own, grads_sib, before = refs[:5]
    outs, total, held_sib, sem = refs[5:9], refs[9], refs[10], refs[11]
    depth = held_sib.shape[0]
    copy = pltpu.make_async_copy(grads_sib.at[pl.ds(first, depth), :], held_sib, sem)
    copy.start()
    tile = 512
    half = tile // 2
    piece = half // 4
    m = 0 if x_first else 1
    product = before[pl.ds(m * tile, tile), :].astype(jnp.float32)
    product += product_rows(rows_own, grads_own, first, m, tile)
    copy.wait()
    product += product_rows(rows_sib, held_sib, 0, m, tile)
    total[...] = product.astype(total.dtype)
    for k in range(4):
        for r in range(2):
            if x_first:
                start = r * half + (info[1] ^ k) * piece
                outs[k][pl.ds(r * piece, piece), :] = total[
                    pl.ds(pl.multiple_of(start, piece), piece), :
                ]
            else:
                inner = (info[2] ^ k) * STRIP
                for xx in range(X_CHIPS):
                    start = pl.multiple_of(r * half + xx * piece + inner, STRIP)
                    outs[k][pl.ds(r * piece + xx * STRIP, STRIP), :] = total[pl.ds(start, STRIP), :]


def make_partial(info, rows_own, rows_sib, grads_own, grads_sib, before, first, x_first):
    width = grads_own.shape[1]
    rows = rows_own.shape[0]
    piece = 128
    vmem = pl.BlockSpec(memory_space=pltpu.VMEM)
    specs = [pl.BlockSpec(memory_space=pltpu.SMEM)] + [vmem] * 5
    specs[4] = pl.BlockSpec(memory_space=pl.ANY)
    return pl.pallas_call(
        functools.partial(partial_kernel, x_first, first * rows),
        in_specs=specs,
        out_specs=[vmem] * 4,
        out_shape=[jax.ShapeDtypeStruct((piece, width), jnp.bfloat16)] * 4,
        scratch_shapes=[
            pltpu.VMEM((512, width), jnp.bfloat16),
            pltpu.VMEM((rows, width), jnp.bfloat16),
            pltpu.SemaphoreType.DMA,
        ],
        compiler_params=params(),
        cost_estimate=pl.CostEstimate(
            flops=4 * rows * width * 512, bytes_accessed=6 * width * 512, transcendentals=0
        ),
        name="partial",
    )(info, rows_own, rows_sib, grads_own, grads_sib, before)


def first_sum_kernel(which, info, *refs):
    pieces, outs, total = refs[:4], refs[4:8], refs[8]
    value = pieces[0][...].astype(jnp.float32)
    for piece in pieces[1:]:
        value += piece[...].astype(jnp.float32)
    total[...] = value.astype(total.dtype)
    half = total.shape[0] // 2
    for k in range(4):
        for r in range(2):
            start = pl.multiple_of(r * half + (info[which] ^ k) * STRIP, STRIP)
            outs[k][pl.ds(r * STRIP, STRIP), :] = total[pl.ds(start, STRIP), :]


def make_first_sum(info, pieces, which):
    rows, width = pieces[0].shape
    vmem = pl.BlockSpec(memory_space=pltpu.VMEM)
    return pl.pallas_call(
        functools.partial(first_sum_kernel, which),
        in_specs=[pl.BlockSpec(memory_space=pltpu.SMEM)] + [vmem] * 4,
        out_specs=[vmem] * 4,
        scratch_shapes=[pltpu.VMEM((rows, width), jnp.bfloat16)],
        out_shape=[jax.ShapeDtypeStruct((2 * STRIP, width), jnp.bfloat16)] * 4,
        compiler_params=params(),
        cost_estimate=pl.CostEstimate(
            flops=4 * rows * width, bytes_accessed=10 * rows * width, transcendentals=0
        ),
        name="first_sum",
    )(info, *pieces)


def second_sum_kernel(col_blocks, listing, *refs):
    pieces, out_ref = refs[:-1], refs[-1]
    block = out_ref.shape[2]
    out_ref[...] = jnp.zeros_like(out_ref)
    for q in range(len(pieces) // 4):
        value = pieces[4 * q][...].astype(jnp.float32)
        for piece in pieces[4 * q + 1 : 4 * q + 4]:
            value += piece[...].astype(jnp.float32)
        value = value.astype(out_ref.dtype)
        for r in range(2):
            for c in range(col_blocks):
                out_ref[listing[(2 * q + r) * col_blocks + c]] = value[
                    r * STRIP : (r + 1) * STRIP, c * block : (c + 1) * block
                ]


def make_second_sum(listing, pieces, slots, block):
    width = pieces[0].shape[1]
    vmem = pl.BlockSpec(memory_space=pltpu.VMEM)
    return pl.pallas_call(
        functools.partial(second_sum_kernel, width // block),
        in_specs=[pl.BlockSpec(memory_space=pltpu.SMEM)] + [vmem] * len(pieces),
        out_specs=vmem,
        out_shape=jax.ShapeDtypeStruct((slots, STRIP, block), jnp.bfloat16),
        compiler_params=params(),
        name="second_sum",
    )(listing, *pieces)


def load_grad(strips_ref, grad_ref):
    for y in range(Y_CHIPS):
        for x in range(X_CHIPS):
            for c in range(CORES):
                start = c * 256 + x * 64 + y * STRIP
                grad_ref[pl.ds(start, STRIP), :] = strips_ref[y * 8 + x * 2 + c]


def direction_kernel(
    owned, strips, moment, second, basis_left, basis_right, direction, moment_out, second_out, grad
):
    @pl.when(owned[0] == 0)
    def _():
        moment_out[...] = moment[...]
        second_out[...] = second[...]
        direction[...] = jnp.zeros_like(direction)

    @pl.when(owned[0] != 0)
    def _():
        load_grad(strips, grad)
        left, right, low = basis_left[...], basis_right[...], grad[...]
        fresh = (
            momentum_decay * moment[...].astype(jnp.float32)
            + (1.0 - momentum_decay) * low.astype(jnp.float32)
        ).astype(jnp.bfloat16)
        moment_out[...] = fresh
        dot = functools.partial(lax.dot_general, preferred_element_type=jnp.float32)
        plain = (((1,), (0,)), ((), ()))
        moment_half = dot(left, fresh, FRONT).astype(jnp.bfloat16)
        grad_half = dot(left, low, FRONT).astype(jnp.bfloat16)
        moment_turned = dot(moment_half, right, plain)
        grad_turned = dot(grad_half, right, plain)
        second_new = (
            factor_decay * second[...].astype(jnp.float32)
            + (1.0 - factor_decay) * grad_turned * grad_turned
        )
        second_out[...] = second_new.astype(jnp.bfloat16)
        scaled = (moment_turned / (jnp.sqrt(second_new) + adam_epsilon)).astype(jnp.bfloat16)
        back_half = dot(left, scaled, plain).astype(jnp.bfloat16)
        update = dot(back_half, right, BACK).astype(jnp.bfloat16)
        for y in range(Y_CHIPS):
            for x in range(X_CHIPS):
                for c in range(CORES):
                    start = x * 128 + c * 64 + y * STRIP
                    direction[y * 8 + x * 2 + c] = update[start : start + STRIP, :]


def make_direction(owned, strips, moment, second, basis_left, basis_right):
    block = moment.shape[0]
    vmem = pl.BlockSpec(memory_space=pltpu.VMEM)
    return pl.pallas_call(
        direction_kernel,
        in_specs=[pl.BlockSpec(memory_space=pltpu.SMEM)] + [vmem] * 5,
        out_specs=[vmem] * 3,
        scratch_shapes=[pltpu.VMEM((block, block), jnp.bfloat16)],
        out_shape=[
            jax.ShapeDtypeStruct(strips.shape, jnp.bfloat16),
            jax.ShapeDtypeStruct(moment.shape, jnp.bfloat16),
            jax.ShapeDtypeStruct(second.shape, jnp.bfloat16),
        ],
        compiler_params=params(),
        cost_estimate=pl.CostEstimate(
            flops=12 * block**3, bytes_accessed=16 * block**2, transcendentals=block**2
        ),
        name="direction",
    )(owned, strips, moment, second, basis_left, basis_right)


def factor_kernel(owned, strips, left, right, left_out, right_out, grad):
    @pl.when(owned[0] == 0)
    def _():
        left_out[...] = left[...]
        right_out[...] = right[...]

    @pl.when(owned[0] != 0)
    def _():
        load_grad(strips, grad)
        low = grad[...]
        dot = functools.partial(lax.dot_general, preferred_element_type=jnp.float32)
        left_out[...] = factor_decay * left[...] + (1.0 - factor_decay) * dot(low, low, BACK)
        right_out[...] = factor_decay * right[...] + (1.0 - factor_decay) * dot(low, low, FRONT)


def make_factors(owned, strips, left, right):
    block = left.shape[0]
    vmem = pl.BlockSpec(memory_space=pltpu.VMEM)
    return pl.pallas_call(
        factor_kernel,
        in_specs=[pl.BlockSpec(memory_space=pltpu.SMEM)] + [vmem] * 3,
        out_specs=[vmem] * 2,
        scratch_shapes=[pltpu.VMEM((block, block), jnp.bfloat16)],
        out_shape=[jax.ShapeDtypeStruct(left.shape, jnp.float32)] * 2,
        compiler_params=params(),
        cost_estimate=pl.CostEstimate(
            flops=4 * block**3, bytes_accessed=18 * block**2, transcendentals=0
        ),
        name="factors",
    )(owned, strips, left, right)


def pick_kernel(col_blocks, info, listing, strips, *outs):
    block = strips.shape[2]
    for k in range(Y_CHIPS):
        r = info[2] ^ k
        for c in range(col_blocks):
            outs[k][:, c * block : (c + 1) * block] = strips[listing[r * col_blocks + c]]


def make_pick(info, listing, strips, col_blocks):
    vmem = pl.BlockSpec(memory_space=pltpu.VMEM)
    smem = pl.BlockSpec(memory_space=pltpu.SMEM)
    width = strips.shape[2] * col_blocks
    return pl.pallas_call(
        functools.partial(pick_kernel, col_blocks),
        in_specs=[smem, smem, vmem],
        out_specs=[vmem] * Y_CHIPS,
        out_shape=[jax.ShapeDtypeStruct((STRIP, width), jnp.bfloat16)] * Y_CHIPS,
        compiler_params=params(),
        name="pick",
    )(info, listing, strips)


def place_kernel(info, *refs):
    pieces, out_ref = refs[:-1], refs[-1]
    for k in range(Y_CHIPS):
        start = (info[2] ^ k) * STRIP
        out_ref[pl.ds(pl.multiple_of(start, STRIP), STRIP), :] = pieces[k][...]


def make_place(info, pieces):
    vmem = pl.BlockSpec(memory_space=pltpu.VMEM)
    rows, width = pieces[0].shape
    return pl.pallas_call(
        place_kernel,
        in_specs=[pl.BlockSpec(memory_space=pltpu.SMEM)] + [vmem] * Y_CHIPS,
        out_specs=vmem,
        out_shape=jax.ShapeDtypeStruct((rows * Y_CHIPS, width), jnp.bfloat16),
        compiler_params=params(),
        name="place",
    )(info, *pieces)


def split_kernel(block, tokens, kept, given):
    half = block // CORES
    core = lax.rem(lax.axis_index("dp"), CORES)
    for r in range(tokens.shape[1] // block):
        for ref, side in ((kept, core), (given, 1 - core)):
            start = pl.multiple_of(r * block + side * half, half)
            ref[:, r * half : (r + 1) * half] = tokens[:, pl.ds(start, half)]


def make_split(tokens, block):
    rows, width = tokens.shape
    vmem = pl.BlockSpec(memory_space=pltpu.VMEM)
    return pl.pallas_call(
        functools.partial(split_kernel, block),
        in_specs=[vmem],
        out_specs=[vmem] * 2,
        out_shape=[jax.ShapeDtypeStruct((rows, width // CORES), tokens.dtype)] * 2,
        compiler_params=params(),
        name="split",
    )(tokens)


def body(
    tokens_in,
    pre_act,
    grad_hidden,
    sample_tokens,
    block_slot,
    moment,
    second,
    left,
    right,
    basis_left,
    basis_right,
):
    place = lax.axis_index("dp")
    at_x, at_y, core = (place // CORES) % X_CHIPS, place // (CORES * X_CHIPS), place % CORES
    at_z = lax.axis_index("mp")
    block = moment.shape[2]
    slots = lax.axis_size("dp")
    listing = block_slot[0]
    info = jnp.stack([at_z, at_x, at_y, core]).astype(jnp.int32)
    own_slot = jnp.any(listing == place).astype(jnp.int32)[None]

    kept, given = make_split(tokens_in, block)
    distance = jnp.array([0, 1, 7, 6, 2, 3, 5, 4], jnp.int32)
    order = (at_z + jnp.where(at_z % 2 == 0, distance, Z_CHIPS - distance)) % Z_CHIPS
    shard_info = jnp.concatenate([order, sample_tokens[0]])

    def pass_on(pair, turn):
        return [lax.ppermute(pair[i], "mp", z_swap((i + turn) % 2)) for i in (0, 1)]

    near_own = pass_on([kept, kept], 0)
    taken = lax.ppermute(given, "dp", core_swap())
    taken, shard_info = lax.optimization_barrier((taken, shard_info))
    near_sib = pass_on([taken, taken], 0)
    grads_own = make_pre_grad(pre_act, grad_hidden, shard_info)
    near_own, grads_own = lax.optimization_barrier((near_own, grads_own))
    middle_own = pass_on(near_own, 1)
    grads_sib = lax.ppermute(grads_own, "dp", core_swap())
    middle_sib = pass_on(near_sib, 1)
    far_own = pass_on(middle_own, 0)
    total = make_gathered(
        [kept, *near_own, *middle_own], [taken, *near_sib], grads_own, grads_sib, 0, 0
    )
    middle_sib, total = lax.optimization_barrier((middle_sib, total))
    far_sib = pass_on(middle_sib, 0)
    last_own = lax.ppermute(far_own[0], "mp", z_swap(1))
    total = make_gathered(far_own, middle_sib, grads_own, grads_sib, 5, 3, total)
    far_sib, total = lax.optimization_barrier((far_sib, total))
    last_sib = lax.ppermute(far_sib[1], "mp", z_swap(0))
    total = make_gathered([], far_sib, grads_own, grads_sib, 0, 5, total)

    swaps = (x_swap, y_swap)
    cut = [
        make_partial(info, last_own, last_sib, grads_own, grads_sib, total, 7, q == 0)
        for q in (0, 1)
    ]
    cut = lax.optimization_barrier(cut)
    strips = []
    for q in (0, 1):
        pieces = [cut[q][0]] + [lax.ppermute(cut[q][k], "dp", swaps[q](k)) for k in (2, 1, 3)]
        seconds = make_first_sum(info, pieces, 2 - q)
        strips += [seconds[0]]
        strips += [lax.ppermute(seconds[k], "dp", swaps[1 - q](k)) for k in (2, 1, 3)]
    outgoing = make_second_sum(listing, strips, slots, block)
    grad_strips = lax.all_to_all(outgoing, "dp", split_axis=0, concat_axis=0, tiled=True)

    direction_strips, moment_out, second_out = make_direction(
        own_slot, grad_strips, moment[0, 0], second[0, 0], basis_left[0, 0], basis_right[0, 0]
    )
    arrived = lax.all_to_all(direction_strips, "dp", split_axis=0, concat_axis=0, tiled=True)
    left_out, right_out = make_factors(own_slot, grad_strips, left[0, 0], right[0, 0])
    picked = make_pick(info, listing, arrived, pre_act.shape[1] // block)
    rows_mine = [picked[0]] + [lax.ppermute(picked[k], "dp", y_swap(k)) for k in (1, 2, 3)]
    direction = make_place(info, rows_mine)
    return (
        direction,
        moment_out[None, None],
        second_out[None, None],
        left_out[None, None],
        right_out[None, None],
    )


def solution(mesh):
    in_specs = (
        P(("dp", "mp"), None),
        P("dp", "mp"),
        P("dp", "mp"),
        P("dp", None),
        P("mp", None),
        P("mp", "dp", None, None),
        P("mp", "dp", None, None),
        P("mp", "dp", None, None),
        P("mp", "dp", None, None),
        P("mp", "dp", None, None),
        P("mp", "dp", None, None),
    )
    out_specs = (
        P("dp", "mp"),
        P("mp", "dp", None, None),
        P("mp", "dp", None, None),
        P("mp", "dp", None, None),
        P("mp", "dp", None, None),
    )
    return jax.shard_map(body, mesh=mesh, in_specs=in_specs, out_specs=out_specs, check_vma=False)
```

profile of v0, /device:TPU:32, one launch (start us, length us, event | category | flops | bytes accessed | tf_op | source)
XLA Modules:
  0.0 136.2 jit_solution(8692897167510436965)
XLA Ops:
  1.7 1.9 %collective-permute-start = (bf16[96,1024]{1,0:T(8,128)(2,1)S(1)}, bf16[96,1024]{1,0:T(8,128)(2,1)S(1)}, u32[]{:S(2)}, u32[]{:S(2)}) collective-permute-start(bf16[96,1024]{1,0:T(8,128)(2,1)S(1)} %get-tuple-element.51.refs_0_), channel_id=1, source_target_pairs={{0,1},{2,3},{4,5},{6,7},{1,0},{3,2},{5,4},{7,6},{8,9},{10,11},{12,... | collective-permute-start | bytes 589832 | tf_op jit(solution)/shard_map/ppermute | solution.py:469
  3.6 2.0 %collective-permute-start.1 = (bf16[96,1024]{1,0:T(8,128)(2,1)S(1)}, bf16[96,1024]{1,0:T(8,128)(2,1)S(1)}, u32[]{:S(2)}, u32[]{:S(2)}) collective-permute-start(bf16[96,1024]{1,0:T(8,128)(2,1)S(1)} %get-tuple-element.51.refs_0_), channel_id=1, source_target_pairs={{1,2},{3,4},{5,6},{7,0},{2,1},{4,3},{6,5},{0,7},{9,10},{11,12},{13... | collective-permute-start | bytes 589832 | tf_op jit(solution)/shard_map/ppermute | solution.py:469
  7.0 1.7 %copy-done.4 = bf16[768,1536]{1,0:T(8,128)(2,1)S(1)} copy-done((bf16[768,1536]{1,0:T(8,128)(2,1)S(1)}, bf16[768,1536]{1,0:T(8,128)(2,1)}, u32[]{:S(2)}) %copy-start.4) | copy-done | bytes 2359320
  8.7 1.7 %copy-done.5 = bf16[768,1536]{1,0:T(8,128)(2,1)S(1)} copy-done((bf16[768,1536]{1,0:T(8,128)(2,1)S(1)}, bf16[768,1536]{1,0:T(8,128)(2,1)}, u32[]{:S(2)}) %copy-start.5) | copy-done | bytes 2359320
  10.4 3.4 %pre_grad.1.refs_8_.refs_4_.refs_2_ = bf16[768,1536]{1,0:T(8,128)(2,1)S(1)} custom-call(s32[11]{0:T(128)S(1)} %pad_add_fusion.1.info, bf16[768,1536]{1,0:T(8,128)(2,1)S(1)} %copy-done.4, bf16[768,1536]{1,0:T(8,128)(2,1)S(1)} %copy-done.5), custom_call_target="tpu_custom_call" | custom-call | flops 47185920 | bytes 7077888 | tf_op jit(solution)/shard_map/pre_grad/pallas_call | solution.py:72
  14.4 3.1 %collective-permute-start.6 = (bf16[96,1024]{1,0:T(8,128)(2,1)S(1)}, bf16[96,1024]{1,0:T(8,128)(2,1)S(1)}, u32[]{:S(2)}, u32[]{:S(2)}) collective-permute-start(bf16[96,1024]{1,0:T(8,128)(2,1)S(1)} %collective-permute-done.2.refs_5_), channel_id=1, source_target_pairs={{0,1},{2,3},{4,5},{6,7},{1,0},{3,2},{5,4},{7,6},{8,9},{10,11},{12,... | collective-permute-start | bytes 589832 | tf_op jit(solution)/shard_map/ppermute | solution.py:469
  20.8 2.4 %collective-permute-done.6.refs_6_ = bf16[96,1024]{1,0:T(8,128)(2,1)S(1)} collective-permute-done((bf16[96,1024]{1,0:T(8,128)(2,1)S(1)}, bf16[96,1024]{1,0:T(8,128)(2,1)S(1)}, u32[]{:S(2)}, u32[]{:S(2)}) %collective-permute-start.6) | collective-permute-done | bytes 196640 | tf_op jit(solution)/shard_map/ppermute | solution.py:469
  26.5 3.0 %collective-permute-done.3.refs_3_ = bf16[96,1024]{1,0:T(8,128)(2,1)S(1)} collective-permute-done((bf16[96,1024]{1,0:T(8,128)(2,1)S(1)}, bf16[96,1024]{1,0:T(8,128)(2,1)S(1)}, u32[]{:S(2)}, u32[]{:S(2)}) %collective-permute-start.3) | collective-permute-done | bytes 196640 | tf_op jit(solution)/shard_map/ppermute | solution.py:469
  31.7 4.0 %gathered.3.refs_6_ = bf16[1024,1536]{1,0:T(8,128)(2,1)S(1)} custom-call(bf16[96,1024]{1,0:T(8,128)(2,1)S(1)} %get-tuple-element.51.refs_0_, bf16[96,1024]{1,0:T(8,128)(2,1)S(1)} %collective-permute-done.refs_1_, bf16[96,1024]{1,0:T(8,128)(2,1)S(1)} %collective-permute-done.1.refs_2_, bf16[96,1024]{1,0:T(8,128)(2,1)S(1)} %collective-permute-done.3.refs_3_, ...), custom_call_target="tpu_custom_call" | custom-call | flops 2415919104 | bytes 6291456 | tf_op jit(solution)/shard_map/gathered/pallas_call | solution.py:140
  38.9 2.2 %gathered.4.refs_4_ = bf16[1024,1536]{1,0:T(8,128)(2,1)S(1)} custom-call(bf16[96,1024]{1,0:T(8,128)(2,1)S(1)} %collective-permute-done.4.refs_0_, bf16[96,1024]{1,0:T(8,128)(2,1)S(1)} %collective-permute-done.14.refs_1_, bf16[96,1024]{1,0:T(8,128)(2,1)S(1)} %collective-permute-done.7.refs_2_, ...), custom_call_target="tpu_custom_call", output_to_operand_aliasing={{}: (6, {})} | custom-call | flops 1207959552 | bytes 6291456 | tf_op jit(solution)/shard_map/gathered/pallas_call | solution.py:140
  43.1 2.6 %collective-permute-start.15 = (bf16[96,1024]{1,0:T(8,128)(2,1)S(1)}, bf16[96,1024]{1,0:T(8,128)(2,1)S(1)}, u32[]{:S(2)}, u32[]{:S(2)}) collective-permute-start(bf16[96,1024]{1,0:T(8,128)(2,1)S(1)} %collective-permute-done.13.refs_1_), channel_id=1, source_target_pairs={{0,1},{2,3},{4,5},{6,7},{1,0},{3,2},{5,4},{7,6},{8,9},{10,11},{12,... | collective-permute-start | bytes 589832 | tf_op jit(solution)/shard_map/ppermute | solution.py:489
  45.8 1.9 %copy-done.1 = bf16[1024,1536]{1,0:T(8,128)(2,1)S(1)} copy-done((bf16[1024,1536]{1,0:T(8,128)(2,1)S(1)}, bf16[1024,1536]{1,0:T(8,128)(2,1)}, u32[]{:S(2)}) %copy-start.1) | copy-done | bytes 3145752
  47.7 1.7 %copy-done.3 = bf16[768,1536]{1,0:T(8,128)(2,1)S(1)} copy-done((bf16[768,1536]{1,0:T(8,128)(2,1)S(1)}, bf16[768,1536]{1,0:T(8,128)(2,1)}, u32[]{:S(2)}) %copy-start.3) | copy-done | bytes 2359320
  50.8 1.8 %partial.3 = (bf16[128,1536]{1,0:T(8,128)(2,1)S(1)}, bf16[128,1536]{1,0:T(8,128)(2,1)S(1)}, bf16[128,1536]{1,0:T(8,128)(2,1)S(1)}, bf16[128,1536]{1,0:T(8,128)(2,1)S(1)}) custom-call(s32[4]{0:T(128)S(1)} %pad_add_fusion.info, bf16[96,1024]{1,0:T(8,128)(2,1)S(1)} %collective-permute-done.5.refs_0_, bf16[96,1024]{1,0:T(8,128)(2,1)S(1)} %collective-permute-done.15.refs_1_, ...), custom_call_target="tpu_custom_call" | custom-call | flops 301989888 | bytes 4718592 | tf_op jit(solution)/shard_map/partial/pallas_call | solution.py:200
  52.6 1.8 %partial.2 = (bf16[128,1536]{1,0:T(8,128)(2,1)S(1)}, bf16[128,1536]{1,0:T(8,128)(2,1)S(1)}, bf16[128,1536]{1,0:T(8,128)(2,1)S(1)}, bf16[128,1536]{1,0:T(8,128)(2,1)S(1)}) custom-call(s32[4]{0:T(128)S(1)} %pad_add_fusion.info, bf16[96,1024]{1,0:T(8,128)(2,1)S(1)} %collective-permute-done.5.refs_0_, bf16[96,1024]{1,0:T(8,128)(2,1)S(1)} %collective-permute-done.15.refs_1_, ...), custom_call_target="tpu_custom_call" | custom-call | flops 301989888 | bytes 4718592 | tf_op jit(solution)/shard_map/partial/pallas_call | solution.py:200
  54.4 3.3 %collective-permute-start.22 = (bf16[128,1536]{1,0:T(8,128)(2,1)S(1)}, bf16[128,1536]{1,0:T(8,128)(2,1)S(1)}, u32[]{:S(2)}, u32[]{:S(2)}) collective-permute-start(bf16[128,1536]{1,0:T(8,128)(2,1)S(1)} %get-tuple-element.81), channel_id=1, source_target_pairs={{0,128},{8,136},{16,144},{24,152},{32,160},{40,168},{48,176},{56,1... | collective-permute-start | bytes 1179656 | tf_op jit(solution)/shard_map/ppermute | solution.py:500
  58.8 3.0 %collective-permute-start.16 = (bf16[128,1536]{1,0:T(8,128)(2,1)S(1)}, bf16[128,1536]{1,0:T(8,128)(2,1)S(1)}, u32[]{:S(2)}, u32[]{:S(2)}) collective-permute-start(bf16[128,1536]{1,0:T(8,128)(2,1)S(1)} %get-tuple-element.73), channel_id=1, source_target_pairs={{0,32},{8,40},{16,48},{24,56},{32,0},{40,8},{48,16},{56,24},{64,96... | collective-permute-start | bytes 1179656 | tf_op jit(solution)/shard_map/ppermute | solution.py:500
  62.4 5.1 %collective-permute-done.22.refs_1_ = bf16[128,1536]{1,0:T(8,128)(2,1)S(1)} collective-permute-done((bf16[128,1536]{1,0:T(8,128)(2,1)S(1)}, bf16[128,1536]{1,0:T(8,128)(2,1)S(1)}, u32[]{:S(2)}, u32[]{:S(2)}) %collective-permute-start.22) | collective-permute-done | bytes 393248 | tf_op jit(solution)/shard_map/ppermute | solution.py:500
  67.4 2.8 %collective-permute-start.18 = (bf16[128,1536]{1,0:T(8,128)(2,1)S(1)}, bf16[128,1536]{1,0:T(8,128)(2,1)S(1)}, u32[]{:S(2)}, u32[]{:S(2)}) collective-permute-start(bf16[128,1536]{1,0:T(8,128)(2,1)S(1)} %get-tuple-element.75), channel_id=1, source_target_pairs={{0,48},{8,56},{16,32},{24,40},{32,16},{40,24},{48,0},{56,8},{64,11... | collective-permute-start | bytes 1179656 | tf_op jit(solution)/shard_map/ppermute | solution.py:500
  70.2 1.8 %collective-permute-done.23.refs_2_ = bf16[128,1536]{1,0:T(8,128)(2,1)S(1)} collective-permute-done((bf16[128,1536]{1,0:T(8,128)(2,1)S(1)}, bf16[128,1536]{1,0:T(8,128)(2,1)S(1)}, u32[]{:S(2)}, u32[]{:S(2)}) %collective-permute-start.23) | collective-permute-done | bytes 393248 | tf_op jit(solution)/shard_map/ppermute | solution.py:500
  73.0 3.1 %collective-permute-start.25 = (bf16[32,1536]{1,0:T(8,128)(2,1)S(1)}, bf16[32,1536]{1,0:T(8,128)(2,1)S(1)}, u32[]{:S(2)}, u32[]{:S(2)}) collective-permute-start(bf16[32,1536]{1,0:T(8,128)(2,1)S(1)} %get-tuple-element.85), channel_id=1, source_target_pairs={{0,32},{8,40},{16,48},{24,56},{32,0},{40,8},{48,16},{56,24},{64,96... | collective-permute-start | bytes 294920 | tf_op jit(solution)/shard_map/ppermute | solution.py:503
  78.4 3.6 %collective-permute-start.19 = (bf16[32,1536]{1,0:T(8,128)(2,1)S(1)}, bf16[32,1536]{1,0:T(8,128)(2,1)S(1)}, u32[]{:S(2)}, u32[]{:S(2)}) collective-permute-start(bf16[32,1536]{1,0:T(8,128)(2,1)S(1)} %get-tuple-element.77), channel_id=1, source_target_pairs={{0,128},{8,136},{16,144},{24,152},{32,160},{40,168},{48,176},{56,1... | collective-permute-start | bytes 294920 | tf_op jit(solution)/shard_map/ppermute | solution.py:503
  82.4 1.6 %collective-permute-start.21 = (bf16[32,1536]{1,0:T(8,128)(2,1)S(1)}, bf16[32,1536]{1,0:T(8,128)(2,1)S(1)}, u32[]{:S(2)}, u32[]{:S(2)}) collective-permute-start(bf16[32,1536]{1,0:T(8,128)(2,1)S(1)} %get-tuple-element.79), channel_id=1, source_target_pairs={{0,192},{8,200},{16,208},{24,216},{32,224},{40,232},{48,240},{56,2... | collective-permute-start | bytes 294920 | tf_op jit(solution)/shard_map/ppermute | solution.py:503
  84.7 1.9 %collective-permute-done.20.refs_2_ = bf16[32,1536]{1,0:T(8,128)(2,1)S(1)} collective-permute-done((bf16[32,1536]{1,0:T(8,128)(2,1)S(1)}, bf16[32,1536]{1,0:T(8,128)(2,1)S(1)}, u32[]{:S(2)}, u32[]{:S(2)}) %collective-permute-start.20) | collective-permute-done | bytes 98336 | tf_op jit(solution)/shard_map/ppermute | solution.py:503
  86.6 1.6 %collective-permute-done.21.refs_3_ = bf16[32,1536]{1,0:T(8,128)(2,1)S(1)} collective-permute-done((bf16[32,1536]{1,0:T(8,128)(2,1)S(1)}, bf16[32,1536]{1,0:T(8,128)(2,1)S(1)}, u32[]{:S(2)}, u32[]{:S(2)}) %collective-permute-start.21) | collective-permute-done | bytes 98336 | tf_op jit(solution)/shard_map/ppermute | solution.py:503
  89.7 6.6 %all-to-all-start = ((bf16[32,16,512]{2,1,0:T(8,128)(2,1)}), bf16[32,16,512]{2,1,0:T(8,128)(2,1)S(1)}, u32[]{:S(2)}, u32[]{:S(2)}) async-start(bf16[32,16,512]{2,1,0:T(8,128)(2,1)} %second_sum.1), calls=%async_computation | async-start | bytes 1048576 | tf_op jit(solution)/shard_map/all_to_all | solution.py:505
  97.7 10.5 %all-to-all-done.strips = bf16[32,16,512]{2,1,0:T(8,128)(2,1)S(1)} async-done(((bf16[32,16,512]{2,1,0:T(8,128)(2,1)}), bf16[32,16,512]{2,1,0:T(8,128)(2,1)S(1)}, u32[]{:S(2)}, u32[]{:S(2)}) %all-to-all-start) | async-done | bytes 524320 | tf_op jit(solution)/shard_map/all_to_all | solution.py:505
  108.2 3.5 %direction.1 = (bf16[32,16,512]{2,1,0:T(8,128)(2,1)S(1)}, bf16[512,512]{1,0:T(8,128)(2,1)}, bf16[512,512]{1,0:T(8,128)(2,1)}) custom-call(s32[1]{0:T(128)} %bitcast.5.owned, bf16[32,16,512]{2,1,0:T(8,128)(2,1)S(1)} %all-to-all-done.strips, bf16[512,512]{1,0:T(8,128)(2,1)S(1)} %bitcast.22, bf16[512,512]{1,0:T(8,128)(2,1)S(1)} %bitcast.23, ...), custom_call_target="tpu_custom_call" | custom-call | flops 1610612736 | bytes 4194304 | tf_op jit(solution)/shard_map/direction/pallas_call | solution.py:327
  111.7 15.1 %all_to_all.10.strips = bf16[32,16,512]{2,1,0:T(8,128)(2,1)S(1)} all-to-all(bf16[32,16,512]{2,1,0:T(8,128)(2,1)S(1)} %get-tuple-element.88), channel_id=1, replica_groups=mesh['dp'=32,'mp'=8] {'dp'}, dimensions={0} | all-to-all | bytes 1048576 | tf_op jit(solution)/shard_map/all_to_all | solution.py:510
  127.4 2.2 %collective-permute-start.29 = (bf16[16,1536]{1,0:T(8,128)(2,1)S(1)}, bf16[16,1536]{1,0:T(8,128)(2,1)S(1)}, u32[]{:S(2)}, u32[]{:S(2)}) collective-permute-start(bf16[16,1536]{1,0:T(8,128)(2,1)S(1)} %get-tuple-element.91), channel_id=1, source_target_pairs={{0,128},{8,136},{16,144},{24,152},{32,160},{40,168},{48,176},{56,1... | collective-permute-start | bytes 147464 | tf_op jit(solution)/shard_map/ppermute | solution.py:513
  129.7 2.5 %collective-permute-start.30 = (bf16[16,1536]{1,0:T(8,128)(2,1)S(1)}, bf16[16,1536]{1,0:T(8,128)(2,1)S(1)}, u32[]{:S(2)}, u32[]{:S(2)}) collective-permute-start(bf16[16,1536]{1,0:T(8,128)(2,1)S(1)} %get-tuple-element.92), channel_id=1, source_target_pairs={{0,192},{8,200},{16,208},{24,216},{32,224},{40,232},{48,240},{56,2... | collective-permute-start | bytes 147464 | tf_op jit(solution)/shard_map/ppermute | solution.py:513
  132.1 2.1 %factors.1 = (f32[512,512]{1,0:T(8,128)}, f32[512,512]{1,0:T(8,128)}) custom-call(s32[1]{0:T(128)} %bitcast.5.owned, bf16[32,16,512]{2,1,0:T(8,128)(2,1)S(1)} %all-to-all-done.strips, f32[512,512]{1,0:T(8,128)S(1)} %bitcast.18, f32[512,512]{1,0:T(8,128)S(1)} %bitcast.19), custom_call_target="tpu_custom_call" | custom-call | flops 536870912 | bytes 4718592 | tf_op jit(solution)/shard_map/factors/pallas_call | solution.py:363
  (79 shorter events, 29.2 us)
Async XLA Ops:
  1.7 12.1 %collective-permute-start = (bf16[96,1024]{1,0:T(8,128)(2,1)S(1)}, bf16[96,1024]{1,0:T(8,128)(2,1)S(1)}, u32[]{:S(2)}, u32[]{:S(2)}) collective-permute-start(bf16[96,1024]{1,0:T(8,128)(2,1)S(1)} %get-tuple-element.51.refs_0_), channel_id=1, source_target_pairs={{0,1},{2,3},{4,5},{6,7},{1,0},{3,2},{5,4},{7,6},{8,9},{10,11},{12,... | collective-permute-start | bytes 589832 | tf_op jit(solution)/shard_map/ppermute | solution.py:469
  3.6 10.2 %collective-permute-start.1 = (bf16[96,1024]{1,0:T(8,128)(2,1)S(1)}, bf16[96,1024]{1,0:T(8,128)(2,1)S(1)}, u32[]{:S(2)}, u32[]{:S(2)}) collective-permute-start(bf16[96,1024]{1,0:T(8,128)(2,1)S(1)} %get-tuple-element.51.refs_0_), channel_id=1, source_target_pairs={{1,2},{3,4},{5,6},{7,0},{2,1},{4,3},{6,5},{0,7},{9,10},{11,12},{13... | collective-permute-start | bytes 589832 | tf_op jit(solution)/shard_map/ppermute | solution.py:469
  5.6 1.4 %collective-permute-start.2 = (bf16[96,1024]{1,0:T(8,128)(2,1)S(1)}, bf16[96,1024]{1,0:T(8,128)(2,1)S(1)}, u32[]{:S(2)}, u32[]{:S(2)}) collective-permute-start(bf16[96,1024]{1,0:T(8,128)(2,1)S(1)} %get-tuple-element.52), channel_id=1, source_target_pairs={{0,8},{8,0},{16,24},{24,16},{32,40},{40,32},{48,56},{56,48},{64,72... | collective-permute-start | bytes 589832 | tf_op jit(solution)/shard_map/ppermute | solution.py:472
  13.8 17.9 %collective-permute-start.11 = (bf16[768,1536]{1,0:T(8,128)(2,1)S(1)}, bf16[768,1536]{1,0:T(8,128)(2,1)S(1)}, u32[]{:S(2)}, u32[]{:S(2)}) collective-permute-start(bf16[768,1536]{1,0:T(8,128)(2,1)S(1)} %pre_grad.1.refs_8_.refs_4_.refs_2_), channel_id=1, source_target_pairs={{0,8},{8,0},{16,24},{24,16},{32,40},{40,32},{48,56},{56,48},{64,72... | collective-permute-start | bytes 7077896 | tf_op jit(solution)/shard_map/ppermute | solution.py:478
  14.4 8.8 %collective-permute-start.6 = (bf16[96,1024]{1,0:T(8,128)(2,1)S(1)}, bf16[96,1024]{1,0:T(8,128)(2,1)S(1)}, u32[]{:S(2)}, u32[]{:S(2)}) collective-permute-start(bf16[96,1024]{1,0:T(8,128)(2,1)S(1)} %collective-permute-done.2.refs_5_), channel_id=1, source_target_pairs={{0,1},{2,3},{4,5},{6,7},{1,0},{3,2},{5,4},{7,6},{8,9},{10,11},{12,... | collective-permute-start | bytes 589832 | tf_op jit(solution)/shard_map/ppermute | solution.py:469
  17.5 7.8 %collective-permute-start.8 = (bf16[96,1024]{1,0:T(8,128)(2,1)S(1)}, bf16[96,1024]{1,0:T(8,128)(2,1)S(1)}, u32[]{:S(2)}, u32[]{:S(2)}) collective-permute-start(bf16[96,1024]{1,0:T(8,128)(2,1)S(1)} %collective-permute-done.2.refs_5_), channel_id=1, source_target_pairs={{1,2},{3,4},{5,6},{7,0},{2,1},{4,3},{6,5},{0,7},{9,10},{11,12},{13... | collective-permute-start | bytes 589832 | tf_op jit(solution)/shard_map/ppermute | solution.py:469
  18.5 11.0 %collective-permute-start.3 = (bf16[96,1024]{1,0:T(8,128)(2,1)S(1)}, bf16[96,1024]{1,0:T(8,128)(2,1)S(1)}, u32[]{:S(2)}, u32[]{:S(2)}) collective-permute-start(bf16[96,1024]{1,0:T(8,128)(2,1)S(1)} %collective-permute-done.refs_1_), channel_id=1, source_target_pairs={{1,2},{3,4},{5,6},{7,0},{2,1},{4,3},{6,5},{0,7},{9,10},{11,12},{13... | collective-permute-start | bytes 589832 | tf_op jit(solution)/shard_map/ppermute | solution.py:469
  19.6 11.1 %collective-permute-start.10 = (bf16[96,1024]{1,0:T(8,128)(2,1)S(1)}, bf16[96,1024]{1,0:T(8,128)(2,1)S(1)}, u32[]{:S(2)}, u32[]{:S(2)}) collective-permute-start(bf16[96,1024]{1,0:T(8,128)(2,1)S(1)} %collective-permute-done.1.refs_2_), channel_id=1, source_target_pairs={{0,1},{2,3},{4,5},{6,7},{1,0},{3,2},{5,4},{7,6},{8,9},{10,11},{12,... | collective-permute-start | bytes 589832 | tf_op jit(solution)/shard_map/ppermute | solution.py:469
  23.2 12.5 %collective-permute-start.7 = (bf16[96,1024]{1,0:T(8,128)(2,1)S(1)}, bf16[96,1024]{1,0:T(8,128)(2,1)S(1)}, u32[]{:S(2)}, u32[]{:S(2)}) collective-permute-start(bf16[96,1024]{1,0:T(8,128)(2,1)S(1)} %collective-permute-done.6.refs_6_), channel_id=1, source_target_pairs={{1,2},{3,4},{5,6},{7,0},{2,1},{4,3},{6,5},{0,7},{9,10},{11,12},{13... | collective-permute-start | bytes 589832 | tf_op jit(solution)/shard_map/ppermute | solution.py:469
  25.3 10.4 %collective-permute-start.9 = (bf16[96,1024]{1,0:T(8,128)(2,1)S(1)}, bf16[96,1024]{1,0:T(8,128)(2,1)S(1)}, u32[]{:S(2)}, u32[]{:S(2)}) collective-permute-start(bf16[96,1024]{1,0:T(8,128)(2,1)S(1)} %collective-permute-done.8.refs_7_), channel_id=1, source_target_pairs={{0,1},{2,3},{4,5},{6,7},{1,0},{3,2},{5,4},{7,6},{8,9},{10,11},{12,... | collective-permute-start | bytes 589832 | tf_op jit(solution)/shard_map/ppermute | solution.py:469
  29.5 8.3 %collective-permute-start.4 = (bf16[96,1024]{1,0:T(8,128)(2,1)S(1)}, bf16[96,1024]{1,0:T(8,128)(2,1)S(1)}, u32[]{:S(2)}, u32[]{:S(2)}) collective-permute-start(bf16[96,1024]{1,0:T(8,128)(2,1)S(1)} %collective-permute-done.3.refs_3_), channel_id=1, source_target_pairs={{0,1},{2,3},{4,5},{6,7},{1,0},{3,2},{5,4},{7,6},{8,9},{10,11},{12,... | collective-permute-start | bytes 589832 | tf_op jit(solution)/shard_map/ppermute | solution.py:469
  30.7 8.2 %collective-permute-start.14 = (bf16[96,1024]{1,0:T(8,128)(2,1)S(1)}, bf16[96,1024]{1,0:T(8,128)(2,1)S(1)}, u32[]{:S(2)}, u32[]{:S(2)}) collective-permute-start(bf16[96,1024]{1,0:T(8,128)(2,1)S(1)} %collective-permute-done.10.refs_4_), channel_id=1, source_target_pairs={{1,2},{3,4},{5,6},{7,0},{2,1},{4,3},{6,5},{0,7},{9,10},{11,12},{13... | collective-permute-start | bytes 589832 | tf_op jit(solution)/shard_map/ppermute | solution.py:469
  35.7 7.0 %collective-permute-start.12 = (bf16[96,1024]{1,0:T(8,128)(2,1)S(1)}, bf16[96,1024]{1,0:T(8,128)(2,1)S(1)}, u32[]{:S(2)}, u32[]{:S(2)}) collective-permute-start(bf16[96,1024]{1,0:T(8,128)(2,1)S(1)} %collective-permute-done.7.refs_2_), channel_id=1, source_target_pairs={{0,1},{2,3},{4,5},{6,7},{1,0},{3,2},{5,4},{7,6},{8,9},{10,11},{12,... | collective-permute-start | bytes 589832 | tf_op jit(solution)/shard_map/ppermute | solution.py:469
  36.9 6.3 %collective-permute-start.13 = (bf16[96,1024]{1,0:T(8,128)(2,1)S(1)}, bf16[96,1024]{1,0:T(8,128)(2,1)S(1)}, u32[]{:S(2)}, u32[]{:S(2)}) collective-permute-start(bf16[96,1024]{1,0:T(8,128)(2,1)S(1)} %collective-permute-done.9.refs_3_), channel_id=1, source_target_pairs={{1,2},{3,4},{5,6},{7,0},{2,1},{4,3},{6,5},{0,7},{9,10},{11,12},{13... | collective-permute-start | bytes 589832 | tf_op jit(solution)/shard_map/ppermute | solution.py:469
  37.9 12.9 %collective-permute-start.5 = (bf16[96,1024]{1,0:T(8,128)(2,1)S(1)}, bf16[96,1024]{1,0:T(8,128)(2,1)S(1)}, u32[]{:S(2)}, u32[]{:S(2)}) collective-permute-start(bf16[96,1024]{1,0:T(8,128)(2,1)S(1)} %collective-permute-done.4.refs_0_), channel_id=1, source_target_pairs={{1,2},{3,4},{5,6},{7,0},{2,1},{4,3},{6,5},{0,7},{9,10},{11,12},{13... | collective-permute-start | bytes 589832 | tf_op jit(solution)/shard_map/ppermute | solution.py:486
  43.1 7.7 %collective-permute-start.15 = (bf16[96,1024]{1,0:T(8,128)(2,1)S(1)}, bf16[96,1024]{1,0:T(8,128)(2,1)S(1)}, u32[]{:S(2)}, u32[]{:S(2)}) collective-permute-start(bf16[96,1024]{1,0:T(8,128)(2,1)S(1)} %collective-permute-done.13.refs_1_), channel_id=1, source_target_pairs={{0,1},{2,3},{4,5},{6,7},{1,0},{3,2},{5,4},{7,6},{8,9},{10,11},{12,... | collective-permute-start | bytes 589832 | tf_op jit(solution)/shard_map/ppermute | solution.py:489
  54.4 13.0 %collective-permute-start.22 = (bf16[128,1536]{1,0:T(8,128)(2,1)S(1)}, bf16[128,1536]{1,0:T(8,128)(2,1)S(1)}, u32[]{:S(2)}, u32[]{:S(2)}) collective-permute-start(bf16[128,1536]{1,0:T(8,128)(2,1)S(1)} %get-tuple-element.81), channel_id=1, source_target_pairs={{0,128},{8,136},{16,144},{24,152},{32,160},{40,168},{48,176},{56,1... | collective-permute-start | bytes 1179656 | tf_op jit(solution)/shard_map/ppermute | solution.py:500
  57.7 14.3 %collective-permute-start.23 = (bf16[128,1536]{1,0:T(8,128)(2,1)S(1)}, bf16[128,1536]{1,0:T(8,128)(2,1)S(1)}, u32[]{:S(2)}, u32[]{:S(2)}) collective-permute-start(bf16[128,1536]{1,0:T(8,128)(2,1)S(1)} %get-tuple-element.82), channel_id=1, source_target_pairs={{0,64},{8,72},{16,80},{24,88},{32,96},{40,104},{48,112},{56,120},{... | collective-permute-start | bytes 1179656 | tf_op jit(solution)/shard_map/ppermute | solution.py:500
  58.4 13.6 %collective-permute-start.24 = (bf16[128,1536]{1,0:T(8,128)(2,1)S(1)}, bf16[128,1536]{1,0:T(8,128)(2,1)S(1)}, u32[]{:S(2)}, u32[]{:S(2)}) collective-permute-start(bf16[128,1536]{1,0:T(8,128)(2,1)S(1)} %get-tuple-element.83), channel_id=1, source_target_pairs={{0,192},{8,200},{16,208},{24,216},{32,224},{40,232},{48,240},{56,2... | collective-permute-start | bytes 1179656 | tf_op jit(solution)/shard_map/ppermute | solution.py:500
  58.8 17.9 %collective-permute-start.16 = (bf16[128,1536]{1,0:T(8,128)(2,1)S(1)}, bf16[128,1536]{1,0:T(8,128)(2,1)S(1)}, u32[]{:S(2)}, u32[]{:S(2)}) collective-permute-start(bf16[128,1536]{1,0:T(8,128)(2,1)S(1)} %get-tuple-element.73), channel_id=1, source_target_pairs={{0,32},{8,40},{16,48},{24,56},{32,0},{40,8},{48,16},{56,24},{64,96... | collective-permute-start | bytes 1179656 | tf_op jit(solution)/shard_map/ppermute | solution.py:500
  61.8 15.5 %collective-permute-start.17 = (bf16[128,1536]{1,0:T(8,128)(2,1)S(1)}, bf16[128,1536]{1,0:T(8,128)(2,1)S(1)}, u32[]{:S(2)}, u32[]{:S(2)}) collective-permute-start(bf16[128,1536]{1,0:T(8,128)(2,1)S(1)} %get-tuple-element.74), channel_id=1, source_target_pairs={{0,16},{8,24},{16,0},{24,8},{32,48},{40,56},{48,32},{56,40},{64,80... | collective-permute-start | bytes 1179656 | tf_op jit(solution)/shard_map/ppermute | solution.py:500
  67.4 10.0 %collective-permute-start.18 = (bf16[128,1536]{1,0:T(8,128)(2,1)S(1)}, bf16[128,1536]{1,0:T(8,128)(2,1)S(1)}, u32[]{:S(2)}, u32[]{:S(2)}) collective-permute-start(bf16[128,1536]{1,0:T(8,128)(2,1)S(1)} %get-tuple-element.75), channel_id=1, source_target_pairs={{0,48},{8,56},{16,32},{24,40},{32,16},{40,24},{48,0},{56,8},{64,11... | collective-permute-start | bytes 1179656 | tf_op jit(solution)/shard_map/ppermute | solution.py:500
  73.0 9.5 %collective-permute-start.25 = (bf16[32,1536]{1,0:T(8,128)(2,1)S(1)}, bf16[32,1536]{1,0:T(8,128)(2,1)S(1)}, u32[]{:S(2)}, u32[]{:S(2)}) collective-permute-start(bf16[32,1536]{1,0:T(8,128)(2,1)S(1)} %get-tuple-element.85), channel_id=1, source_target_pairs={{0,32},{8,40},{16,48},{24,56},{32,0},{40,8},{48,16},{56,24},{64,96... | collective-permute-start | bytes 294920 | tf_op jit(solution)/shard_map/ppermute | solution.py:503
  76.1 8.0 %collective-permute-start.26 = (bf16[32,1536]{1,0:T(8,128)(2,1)S(1)}, bf16[32,1536]{1,0:T(8,128)(2,1)S(1)}, u32[]{:S(2)}, u32[]{:S(2)}) collective-permute-start(bf16[32,1536]{1,0:T(8,128)(2,1)S(1)} %get-tuple-element.86), channel_id=1, source_target_pairs={{0,16},{8,24},{16,0},{24,8},{32,48},{40,56},{48,32},{56,40},{64,80... | collective-permute-start | bytes 294920 | tf_op jit(solution)/shard_map/ppermute | solution.py:503
  76.7 7.4 %collective-permute-start.27 = (bf16[32,1536]{1,0:T(8,128)(2,1)S(1)}, bf16[32,1536]{1,0:T(8,128)(2,1)S(1)}, u32[]{:S(2)}, u32[]{:S(2)}) collective-permute-start(bf16[32,1536]{1,0:T(8,128)(2,1)S(1)} %get-tuple-element.87), channel_id=1, source_target_pairs={{0,48},{8,56},{16,32},{24,40},{32,16},{40,24},{48,0},{56,8},{64,11... | collective-permute-start | bytes 294920 | tf_op jit(solution)/shard_map/ppermute | solution.py:503
  78.4 6.3 %collective-permute-start.19 = (bf16[32,1536]{1,0:T(8,128)(2,1)S(1)}, bf16[32,1536]{1,0:T(8,128)(2,1)S(1)}, u32[]{:S(2)}, u32[]{:S(2)}) collective-permute-start(bf16[32,1536]{1,0:T(8,128)(2,1)S(1)} %get-tuple-element.77), channel_id=1, source_target_pairs={{0,128},{8,136},{16,144},{24,152},{32,160},{40,168},{48,176},{56,1... | collective-permute-start | bytes 294920 | tf_op jit(solution)/shard_map/ppermute | solution.py:503
  82.0 4.6 %collective-permute-start.20 = (bf16[32,1536]{1,0:T(8,128)(2,1)S(1)}, bf16[32,1536]{1,0:T(8,128)(2,1)S(1)}, u32[]{:S(2)}, u32[]{:S(2)}) collective-permute-start(bf16[32,1536]{1,0:T(8,128)(2,1)S(1)} %get-tuple-element.78), channel_id=1, source_target_pairs={{0,64},{8,72},{16,80},{24,88},{32,96},{40,104},{48,112},{56,120},{... | collective-permute-start | bytes 294920 | tf_op jit(solution)/shard_map/ppermute | solution.py:503
  82.4 5.8 %collective-permute-start.21 = (bf16[32,1536]{1,0:T(8,128)(2,1)S(1)}, bf16[32,1536]{1,0:T(8,128)(2,1)S(1)}, u32[]{:S(2)}, u32[]{:S(2)}) collective-permute-start(bf16[32,1536]{1,0:T(8,128)(2,1)S(1)} %get-tuple-element.79), channel_id=1, source_target_pairs={{0,192},{8,200},{16,208},{24,216},{32,224},{40,232},{48,240},{56,2... | collective-permute-start | bytes 294920 | tf_op jit(solution)/shard_map/ppermute | solution.py:503
  89.7 18.4 %all-to-all-start = ((bf16[32,16,512]{2,1,0:T(8,128)(2,1)}), bf16[32,16,512]{2,1,0:T(8,128)(2,1)S(1)}, u32[]{:S(2)}, u32[]{:S(2)}) async-start(bf16[32,16,512]{2,1,0:T(8,128)(2,1)} %second_sum.1), calls=%async_computation | async-start | bytes 1048576 | tf_op jit(solution)/shard_map/all_to_all | solution.py:505
  127.3 6.9 %collective-permute-start.28 = (bf16[16,1536]{1,0:T(8,128)(2,1)S(1)}, bf16[16,1536]{1,0:T(8,128)(2,1)S(1)}, u32[]{:S(2)}, u32[]{:S(2)}) collective-permute-start(bf16[16,1536]{1,0:T(8,128)(2,1)S(1)} %get-tuple-element.90), channel_id=1, source_target_pairs={{0,64},{8,72},{16,80},{24,88},{32,96},{40,104},{48,112},{56,120},{... | collective-permute-start | bytes 147464 | tf_op jit(solution)/shard_map/ppermute | solution.py:513
  127.4 6.8 %collective-permute-start.29 = (bf16[16,1536]{1,0:T(8,128)(2,1)S(1)}, bf16[16,1536]{1,0:T(8,128)(2,1)S(1)}, u32[]{:S(2)}, u32[]{:S(2)}) collective-permute-start(bf16[16,1536]{1,0:T(8,128)(2,1)S(1)} %get-tuple-element.91), channel_id=1, source_target_pairs={{0,128},{8,136},{16,144},{24,152},{32,160},{40,168},{48,176},{56,1... | collective-permute-start | bytes 147464 | tf_op jit(solution)/shard_map/ppermute | solution.py:513
  129.7 5.3 %collective-permute-start.30 = (bf16[16,1536]{1,0:T(8,128)(2,1)S(1)}, bf16[16,1536]{1,0:T(8,128)(2,1)S(1)}, u32[]{:S(2)}, u32[]{:S(2)}) collective-permute-start(bf16[16,1536]{1,0:T(8,128)(2,1)S(1)} %get-tuple-element.92), channel_id=1, source_target_pairs={{0,192},{8,200},{16,208},{24,216},{32,224},{40,232},{48,240},{56,2... | collective-permute-start | bytes 147464 | tf_op jit(solution)/shard_map/ppermute | solution.py:513
  (14 other events, 239.2 us)
where the time goes:
time: 137 us; the launch traced here: 136 us
  starting transfers between devices  53 us (39%)
  waiting for transfers between devices  29.5 us (22%)
  Pallas kernels  25.4 us (19%)
  blocking collectives  15.1 us (11%)
  local copies, waits for them, and re-layouts  9.53 us (7%)
  other arithmetic  2.11 us (2%)
  between operations  1.54 us (1%)
    ppermute x12, starting transfers between devices, pass_on(): return [lax.ppermute(pair[i], 'mp', z_swap((i + turn) % 2)) for i in (0, 1)]  16.8 us
    all_to_all x1, blocking collectives, body(): lax.all_to_all(direction_strips, 'dp', split_axis=0, concat_axis=0, tiled...  15.1 us
    ppermute x6, starting transfers between devices, body(): lax.ppermute(cut[q][k], 'dp', swaps[q](k))  10.7 us
    all_to_all x1, waiting for transfers between devices, body(): lax.all_to_all(outgoing, 'dp', split_axis=0, concat_axis=0, tiled=True)  10.5 us
    ppermute x6, starting transfers between devices, body(): lax.ppermute(seconds[k], 'dp', swaps[1 - q](k))  9.89 us
    unnamed x28, local copies, waits for them, and re-layouts  9.53 us
    pallas_call x3, Pallas kernels, make_gathered(): pl.pallas_call(functools.partial(gather_kernel, len(own), len(sib), first...  7.57 us
    ppermute x6, waiting for transfers between devices, body(): lax.ppermute(cut[q][k], 'dp', swaps[q](k))  7.08 us
  transfers between devices with their start and end apart: 32, of which 12 were waited for; matrix products, arithmetic and copies ran while one was open for 2% of the time, Pallas kernels for 11%

commit v1 on v0

--- a/solution.py
+++ b/solution.py
@@ -490,17 +490,13 @@
     total = make_gathered([], far_sib, grads_own, grads_sib, 0, 5, total)
 
     swaps = (x_swap, y_swap)
-    cut = [
-        make_partial(info, last_own, last_sib, grads_own, grads_sib, total, 7, q == 0)
-        for q in (0, 1)
-    ]
-    cut = lax.optimization_barrier(cut)
     strips = []
     for q in (0, 1):
-        pieces = [cut[q][0]] + [lax.ppermute(cut[q][k], "dp", swaps[q](k)) for k in (2, 1, 3)]
+        pieces = make_partial(info, last_own, last_sib, grads_own, grads_sib, total, 7, q == 0)
+        pieces = [pieces[0]] + [lax.ppermute(pieces[k], "dp", swaps[q](k)) for k in (1, 3, 2)]
         seconds = make_first_sum(info, pieces, 2 - q)
         strips += [seconds[0]]
-        strips += [lax.ppermute(seconds[k], "dp", swaps[1 - q](k)) for k in (2, 1, 3)]
+        strips += [lax.ppermute(seconds[k], "dp", swaps[1 - q](k)) for k in (1, 3, 2)]
     outgoing = make_second_sum(listing, strips, slots, block)
     grad_strips = lax.all_to_all(outgoing, "dp", split_axis=0, concat_axis=0, tiled=True)
 

time: 137 us -> 135 us (0.985)
  starting transfers between devices: 53 us -> 49.8 us
  waiting for transfers between devices: 29.5 us -> 31 us
    all_to_all x1, starting transfers between devices: 6.65 us -> 4.21 us  [body(): lax.all_to_all(outgoing, 'dp', split_axis=0, concat_axis=0, tiled=True)]
    ppermute x6, starting transfers between devices: 9.89 us -> 8.5 us  [body(): lax.ppermute(seconds[k], 'dp', swaps[1 - q](k))]
  transfers between devices with their start and end apart: 32 -> 32, of which waited for: 12 -> 13; matrix products, arithmetic and copies ran while one was open for 2% -> 2% of each run, Pallas kernels for 11% -> 12%
where the time goes in v1:
time: 135 us
  starting transfers between devices  49.8 us (37%)
  waiting for transfers between devices  31 us (23%)
  Pallas kernels  25.4 us (19%)
  blocking collectives  15.2 us (11%)
  local copies, waits for them, and re-layouts  9.53 us (7%)
  other arithmetic  2.11 us (2%)
  between operations  1.54 us (1%)
    ppermute x12, starting transfers between devices, pass_on(): return [lax.ppermute(pair[i], 'mp', z_swap((i + turn) % 2)) for i in (0, 1)]  16.8 us
    all_to_all x1, blocking collectives, body(): lax.all_to_all(direction_strips, 'dp', split_axis=0, concat_axis=0, tiled...  15.2 us
    ppermute x6, starting transfers between devices, body(): lax.ppermute(pieces[k], 'dp', swaps[q](k))  11.3 us
    all_to_all x1, waiting for transfers between devices, body(): lax.all_to_all(outgoing, 'dp', split_axis=0, concat_axis=0, tiled=True)  10.5 us
    unnamed x28, local copies, waits for them, and re-layouts  9.53 us
    ppermute x6, starting transfers between devices, body(): lax.ppermute(seconds[k], 'dp', swaps[1 - q](k))  8.5 us
    pallas_call x3, Pallas kernels, make_gathered(): pl.pallas_call(functools.partial(gather_kernel, len(own), len(sib), first...  7.57 us
    ppermute x6, waiting for transfers between devices, body(): lax.ppermute(pieces[k], 'dp', swaps[q](k))  7.54 us
  transfers between devices with their start and end apart: 32, of which 13 were waited for; matrix products, arithmetic and copies ran while one was open for 2% of the time, Pallas kernels for 12%

profile of v1, /device:TPU:32, one launch (start us, length us, event | category | flops | bytes accessed | tf_op | source)
XLA Modules:
  0.0 134.6 jit_solution(6492367882136832222)
XLA Ops:
  1.7 1.9 %collective-permute-start = (bf16[96,1024]{1,0:T(8,128)(2,1)S(1)}, bf16[96,1024]{1,0:T(8,128)(2,1)S(1)}, u32[]{:S(2)}, u32[]{:S(2)}) collective-permute-start(bf16[96,1024]{1,0:T(8,128)(2,1)S(1)} %get-tuple-element.43.refs_0_), channel_id=1, source_target_pairs={{0,1},{2,3},{4,5},{6,7},{1,0},{3,2},{5,4},{7,6},{8,9},{10,11},{12,... | collective-permute-start | bytes 589832 | tf_op jit(solution)/shard_map/ppermute | solution.py:469
  3.6 2.0 %collective-permute-start.1 = (bf16[96,1024]{1,0:T(8,128)(2,1)S(1)}, bf16[96,1024]{1,0:T(8,128)(2,1)S(1)}, u32[]{:S(2)}, u32[]{:S(2)}) collective-permute-start(bf16[96,1024]{1,0:T(8,128)(2,1)S(1)} %get-tuple-element.43.refs_0_), channel_id=1, source_target_pairs={{1,2},{3,4},{5,6},{7,0},{2,1},{4,3},{6,5},{0,7},{9,10},{11,12},{13... | collective-permute-start | bytes 589832 | tf_op jit(solution)/shard_map/ppermute | solution.py:469
  7.0 1.7 %copy-done.4 = bf16[768,1536]{1,0:T(8,128)(2,1)S(1)} copy-done((bf16[768,1536]{1,0:T(8,128)(2,1)S(1)}, bf16[768,1536]{1,0:T(8,128)(2,1)}, u32[]{:S(2)}) %copy-start.4) | copy-done | bytes 2359320
  8.7 1.7 %copy-done.5 = bf16[768,1536]{1,0:T(8,128)(2,1)S(1)} copy-done((bf16[768,1536]{1,0:T(8,128)(2,1)S(1)}, bf16[768,1536]{1,0:T(8,128)(2,1)}, u32[]{:S(2)}) %copy-start.5) | copy-done | bytes 2359320
  10.4 3.4 %pre_grad.1.refs_8_.refs_4_.refs_2_ = bf16[768,1536]{1,0:T(8,128)(2,1)S(1)} custom-call(s32[11]{0:T(128)S(1)} %pad_add_fusion.1.info, bf16[768,1536]{1,0:T(8,128)(2,1)S(1)} %copy-done.4, bf16[768,1536]{1,0:T(8,128)(2,1)S(1)} %copy-done.5), custom_call_target="tpu_custom_call" | custom-call | flops 47185920 | bytes 7077888 | tf_op jit(solution)/shard_map/pre_grad/pallas_call | solution.py:72
  14.4 3.1 %collective-permute-start.6 = (bf16[96,1024]{1,0:T(8,128)(2,1)S(1)}, bf16[96,1024]{1,0:T(8,128)(2,1)S(1)}, u32[]{:S(2)}, u32[]{:S(2)}) collective-permute-start(bf16[96,1024]{1,0:T(8,128)(2,1)S(1)} %collective-permute-done.2.refs_5_), channel_id=1, source_target_pairs={{0,1},{2,3},{4,5},{6,7},{1,0},{3,2},{5,4},{7,6},{8,9},{10,11},{12,... | collective-permute-start | bytes 589832 | tf_op jit(solution)/shard_map/ppermute | solution.py:469
  20.8 2.4 %collective-permute-done.6.refs_6_ = bf16[96,1024]{1,0:T(8,128)(2,1)S(1)} collective-permute-done((bf16[96,1024]{1,0:T(8,128)(2,1)S(1)}, bf16[96,1024]{1,0:T(8,128)(2,1)S(1)}, u32[]{:S(2)}, u32[]{:S(2)}) %collective-permute-start.6) | collective-permute-done | bytes 196640 | tf_op jit(solution)/shard_map/ppermute | solution.py:469
  26.5 3.0 %collective-permute-done.3.refs_3_ = bf16[96,1024]{1,0:T(8,128)(2,1)S(1)} collective-permute-done((bf16[96,1024]{1,0:T(8,128)(2,1)S(1)}, bf16[96,1024]{1,0:T(8,128)(2,1)S(1)}, u32[]{:S(2)}, u32[]{:S(2)}) %collective-permute-start.3) | collective-permute-done | bytes 196640 | tf_op jit(solution)/shard_map/ppermute | solution.py:469
  31.7 4.0 %gathered.3.refs_6_ = bf16[1024,1536]{1,0:T(8,128)(2,1)S(1)} custom-call(bf16[96,1024]{1,0:T(8,128)(2,1)S(1)} %get-tuple-element.43.refs_0_, bf16[96,1024]{1,0:T(8,128)(2,1)S(1)} %collective-permute-done.refs_1_, bf16[96,1024]{1,0:T(8,128)(2,1)S(1)} %collective-permute-done.1.refs_2_, bf16[96,1024]{1,0:T(8,128)(2,1)S(1)} %collective-permute-done.3.refs_3_, ...), custom_call_target="tpu_custom_call" | custom-call | flops 2415919104 | bytes 6291456 | tf_op jit(solution)/shard_map/gathered/pallas_call | solution.py:140
  38.9 2.2 %gathered.4.refs_4_ = bf16[1024,1536]{1,0:T(8,128)(2,1)S(1)} custom-call(bf16[96,1024]{1,0:T(8,128)(2,1)S(1)} %collective-permute-done.4.refs_0_, bf16[96,1024]{1,0:T(8,128)(2,1)S(1)} %collective-permute-done.14.refs_1_, bf16[96,1024]{1,0:T(8,128)(2,1)S(1)} %collective-permute-done.7.refs_2_, ...), custom_call_target="tpu_custom_call", output_to_operand_aliasing={{}: (6, {})} | custom-call | flops 1207959552 | bytes 6291456 | tf_op jit(solution)/shard_map/gathered/pallas_call | solution.py:140
  43.1 2.6 %collective-permute-start.15 = (bf16[96,1024]{1,0:T(8,128)(2,1)S(1)}, bf16[96,1024]{1,0:T(8,128)(2,1)S(1)}, u32[]{:S(2)}, u32[]{:S(2)}) collective-permute-start(bf16[96,1024]{1,0:T(8,128)(2,1)S(1)} %collective-permute-done.13.refs_1_), channel_id=1, source_target_pairs={{0,1},{2,3},{4,5},{6,7},{1,0},{3,2},{5,4},{7,6},{8,9},{10,11},{12,... | collective-permute-start | bytes 589832 | tf_op jit(solution)/shard_map/ppermute | solution.py:489
  45.8 1.9 %copy-done.1 = bf16[1024,1536]{1,0:T(8,128)(2,1)S(1)} copy-done((bf16[1024,1536]{1,0:T(8,128)(2,1)S(1)}, bf16[1024,1536]{1,0:T(8,128)(2,1)}, u32[]{:S(2)}) %copy-start.1) | copy-done | bytes 3145752
  47.7 1.7 %copy-done.3 = bf16[768,1536]{1,0:T(8,128)(2,1)S(1)} copy-done((bf16[768,1536]{1,0:T(8,128)(2,1)S(1)}, bf16[768,1536]{1,0:T(8,128)(2,1)}, u32[]{:S(2)}) %copy-start.3) | copy-done | bytes 2359320
  50.8 1.8 %partial.3 = (bf16[128,1536]{1,0:T(8,128)(2,1)S(1)}, bf16[128,1536]{1,0:T(8,128)(2,1)S(1)}, bf16[128,1536]{1,0:T(8,128)(2,1)S(1)}, bf16[128,1536]{1,0:T(8,128)(2,1)S(1)}) custom-call(s32[4]{0:T(128)S(1)} %pad_add_fusion.info, bf16[96,1024]{1,0:T(8,128)(2,1)S(1)} %collective-permute-done.5.refs_0_, bf16[96,1024]{1,0:T(8,128)(2,1)S(1)} %collective-permute-done.15.refs_1_, ...), custom_call_target="tpu_custom_call" | custom-call | flops 301989888 | bytes 4718592 | tf_op jit(solution)/shard_map/partial/pallas_call | solution.py:200
  52.6 1.7 %collective-permute-start.22 = (bf16[128,1536]{1,0:T(8,128)(2,1)S(1)}, bf16[128,1536]{1,0:T(8,128)(2,1)S(1)}, u32[]{:S(2)}, u32[]{:S(2)}) collective-permute-start(bf16[128,1536]{1,0:T(8,128)(2,1)S(1)} %get-tuple-element.65), channel_id=1, source_target_pairs={{0,64},{8,72},{16,80},{24,88},{32,96},{40,104},{48,112},{56,120},{... | collective-permute-start | bytes 1179656 | tf_op jit(solution)/shard_map/ppermute | solution.py:496
  54.3 2.2 %collective-permute-start.23 = (bf16[128,1536]{1,0:T(8,128)(2,1)S(1)}, bf16[128,1536]{1,0:T(8,128)(2,1)S(1)}, u32[]{:S(2)}, u32[]{:S(2)}) collective-permute-start(bf16[128,1536]{1,0:T(8,128)(2,1)S(1)} %get-tuple-element.66), channel_id=1, source_target_pairs={{0,192},{8,200},{16,208},{24,216},{32,224},{40,232},{48,240},{56,2... | collective-permute-start | bytes 1179656 | tf_op jit(solution)/shard_map/ppermute | solution.py:496
  57.2 1.8 %partial.2 = (bf16[128,1536]{1,0:T(8,128)(2,1)S(1)}, bf16[128,1536]{1,0:T(8,128)(2,1)S(1)}, bf16[128,1536]{1,0:T(8,128)(2,1)S(1)}, bf16[128,1536]{1,0:T(8,128)(2,1)S(1)}) custom-call(s32[4]{0:T(128)S(1)} %pad_add_fusion.info, bf16[96,1024]{1,0:T(8,128)(2,1)S(1)} %collective-permute-done.5.refs_0_, bf16[96,1024]{1,0:T(8,128)(2,1)S(1)} %collective-permute-done.15.refs_1_, ...), custom_call_target="tpu_custom_call" | custom-call | flops 301989888 | bytes 4718592 | tf_op jit(solution)/shard_map/partial/pallas_call | solution.py:200
  60.6 2.1 %collective-permute-start.17 = (bf16[128,1536]{1,0:T(8,128)(2,1)S(1)}, bf16[128,1536]{1,0:T(8,128)(2,1)S(1)}, u32[]{:S(2)}, u32[]{:S(2)}) collective-permute-start(bf16[128,1536]{1,0:T(8,128)(2,1)S(1)} %get-tuple-element.58), channel_id=1, source_target_pairs={{0,48},{8,56},{16,32},{24,40},{32,16},{40,24},{48,0},{56,8},{64,11... | collective-permute-start | bytes 1179656 | tf_op jit(solution)/shard_map/ppermute | solution.py:496
  64.0 3.0 %collective-permute-start.18 = (bf16[128,1536]{1,0:T(8,128)(2,1)S(1)}, bf16[128,1536]{1,0:T(8,128)(2,1)S(1)}, u32[]{:S(2)}, u32[]{:S(2)}) collective-permute-start(bf16[128,1536]{1,0:T(8,128)(2,1)S(1)} %get-tuple-element.59), channel_id=1, source_target_pairs={{0,32},{8,40},{16,48},{24,56},{32,0},{40,8},{48,16},{56,24},{64,96... | collective-permute-start | bytes 1179656 | tf_op jit(solution)/shard_map/ppermute | solution.py:496
  67.1 3.8 %collective-permute-done.23.refs_2_ = bf16[128,1536]{1,0:T(8,128)(2,1)S(1)} collective-permute-done((bf16[128,1536]{1,0:T(8,128)(2,1)S(1)}, bf16[128,1536]{1,0:T(8,128)(2,1)S(1)}, u32[]{:S(2)}, u32[]{:S(2)}) %collective-permute-start.23) | collective-permute-done | bytes 393248 | tf_op jit(solution)/shard_map/ppermute | solution.py:496
  73.4 2.1 %collective-permute-start.26 = (bf16[32,1536]{1,0:T(8,128)(2,1)S(1)}, bf16[32,1536]{1,0:T(8,128)(2,1)S(1)}, u32[]{:S(2)}, u32[]{:S(2)}) collective-permute-start(bf16[32,1536]{1,0:T(8,128)(2,1)S(1)} %get-tuple-element.70), channel_id=1, source_target_pairs={{0,48},{8,56},{16,32},{24,40},{32,16},{40,24},{48,0},{56,8},{64,11... | collective-permute-start | bytes 294920 | tf_op jit(solution)/shard_map/ppermute | solution.py:499
  76.8 1.8 %collective-permute-done.18.refs_3_ = bf16[128,1536]{1,0:T(8,128)(2,1)S(1)} collective-permute-done((bf16[128,1536]{1,0:T(8,128)(2,1)S(1)}, bf16[128,1536]{1,0:T(8,128)(2,1)S(1)}, u32[]{:S(2)}, u32[]{:S(2)}) %collective-permute-start.18) | collective-permute-done | bytes 393248 | tf_op jit(solution)/shard_map/ppermute | solution.py:496
  80.6 2.2 %collective-permute-start.20 = (bf16[32,1536]{1,0:T(8,128)(2,1)S(1)}, bf16[32,1536]{1,0:T(8,128)(2,1)S(1)}, u32[]{:S(2)}, u32[]{:S(2)}) collective-permute-start(bf16[32,1536]{1,0:T(8,128)(2,1)S(1)} %get-tuple-element.62), channel_id=1, source_target_pairs={{0,192},{8,200},{16,208},{24,216},{32,224},{40,232},{48,240},{56,2... | collective-permute-start | bytes 294920 | tf_op jit(solution)/shard_map/ppermute | solution.py:499
  84.2 2.2 %collective-permute-done.20.refs_2_ = bf16[32,1536]{1,0:T(8,128)(2,1)S(1)} collective-permute-done((bf16[32,1536]{1,0:T(8,128)(2,1)S(1)}, bf16[32,1536]{1,0:T(8,128)(2,1)S(1)}, u32[]{:S(2)}, u32[]{:S(2)}) %collective-permute-start.20) | collective-permute-done | bytes 98336 | tf_op jit(solution)/shard_map/ppermute | solution.py:499
  86.4 2.5 %collective-permute-done.21.refs_3_ = bf16[32,1536]{1,0:T(8,128)(2,1)S(1)} collective-permute-done((bf16[32,1536]{1,0:T(8,128)(2,1)S(1)}, bf16[32,1536]{1,0:T(8,128)(2,1)S(1)}, u32[]{:S(2)}, u32[]{:S(2)}) %collective-permute-start.21) | collective-permute-done | bytes 98336 | tf_op jit(solution)/shard_map/ppermute | solution.py:499
  90.4 4.2 %all-to-all-start = ((bf16[32,16,512]{2,1,0:T(8,128)(2,1)}), bf16[32,16,512]{2,1,0:T(8,128)(2,1)S(1)}, u32[]{:S(2)}, u32[]{:S(2)}) async-start(bf16[32,16,512]{2,1,0:T(8,128)(2,1)} %second_sum.1), calls=%async_computation | async-start | bytes 1048576 | tf_op jit(solution)/shard_map/all_to_all | solution.py:501
  95.9 10.5 %all-to-all-done.strips = bf16[32,16,512]{2,1,0:T(8,128)(2,1)S(1)} async-done(((bf16[32,16,512]{2,1,0:T(8,128)(2,1)}), bf16[32,16,512]{2,1,0:T(8,128)(2,1)S(1)}, u32[]{:S(2)}, u32[]{:S(2)}) %all-to-all-start) | async-done | bytes 524320 | tf_op jit(solution)/shard_map/all_to_all | solution.py:501
  106.4 3.5 %direction.1 = (bf16[32,16,512]{2,1,0:T(8,128)(2,1)S(1)}, bf16[512,512]{1,0:T(8,128)(2,1)}, bf16[512,512]{1,0:T(8,128)(2,1)}) custom-call(s32[1]{0:T(128)} %bitcast.5.owned, bf16[32,16,512]{2,1,0:T(8,128)(2,1)S(1)} %all-to-all-done.strips, bf16[512,512]{1,0:T(8,128)(2,1)S(1)} %bitcast.22, bf16[512,512]{1,0:T(8,128)(2,1)S(1)} %bitcast.23, ...), custom_call_target="tpu_custom_call" | custom-call | flops 1610612736 | bytes 4194304 | tf_op jit(solution)/shard_map/direction/pallas_call | solution.py:327
  109.9 15.2 %all_to_all.10.strips = bf16[32,16,512]{2,1,0:T(8,128)(2,1)S(1)} all-to-all(bf16[32,16,512]{2,1,0:T(8,128)(2,1)S(1)} %get-tuple-element.72), channel_id=1, replica_groups=mesh['dp'=32,'mp'=8] {'dp'}, dimensions={0} | all-to-all | bytes 1048576 | tf_op jit(solution)/shard_map/all_to_all | solution.py:506
  125.8 2.2 %collective-permute-start.29 = (bf16[16,1536]{1,0:T(8,128)(2,1)S(1)}, bf16[16,1536]{1,0:T(8,128)(2,1)S(1)}, u32[]{:S(2)}, u32[]{:S(2)}) collective-permute-start(bf16[16,1536]{1,0:T(8,128)(2,1)S(1)} %get-tuple-element.75), channel_id=1, source_target_pairs={{0,128},{8,136},{16,144},{24,152},{32,160},{40,168},{48,176},{56,1... | collective-permute-start | bytes 147464 | tf_op jit(solution)/shard_map/ppermute | solution.py:509
  128.0 2.5 %collective-permute-start.30 = (bf16[16,1536]{1,0:T(8,128)(2,1)S(1)}, bf16[16,1536]{1,0:T(8,128)(2,1)S(1)}, u32[]{:S(2)}, u32[]{:S(2)}) collective-permute-start(bf16[16,1536]{1,0:T(8,128)(2,1)S(1)} %get-tuple-element.76), channel_id=1, source_target_pairs={{0,192},{8,200},{16,208},{24,216},{32,224},{40,232},{48,240},{56,2... | collective-permute-start | bytes 147464 | tf_op jit(solution)/shard_map/ppermute | solution.py:509
  130.5 2.1 %factors.1 = (f32[512,512]{1,0:T(8,128)}, f32[512,512]{1,0:T(8,128)}) custom-call(s32[1]{0:T(128)} %bitcast.5.owned, bf16[32,16,512]{2,1,0:T(8,128)(2,1)S(1)} %all-to-all-done.strips, f32[512,512]{1,0:T(8,128)S(1)} %bitcast.18, f32[512,512]{1,0:T(8,128)S(1)} %bitcast.19), custom_call_target="tpu_custom_call" | custom-call | flops 536870912 | bytes 4718592 | tf_op jit(solution)/shard_map/factors/pallas_call | solution.py:363
  (79 shorter events, 34.0 us)
Async XLA Ops:
  1.7 12.1 %collective-permute-start = (bf16[96,1024]{1,0:T(8,128)(2,1)S(1)}, bf16[96,1024]{1,0:T(8,128)(2,1)S(1)}, u32[]{:S(2)}, u32[]{:S(2)}) collective-permute-start(bf16[96,1024]{1,0:T(8,128)(2,1)S(1)} %get-tuple-element.43.refs_0_), channel_id=1, source_target_pairs={{0,1},{2,3},{4,5},{6,7},{1,0},{3,2},{5,4},{7,6},{8,9},{10,11},{12,... | collective-permute-start | bytes 589832 | tf_op jit(solution)/shard_map/ppermute | solution.py:469
  3.6 10.2 %collective-permute-start.1 = (bf16[96,1024]{1,0:T(8,128)(2,1)S(1)}, bf16[96,1024]{1,0:T(8,128)(2,1)S(1)}, u32[]{:S(2)}, u32[]{:S(2)}) collective-permute-start(bf16[96,1024]{1,0:T(8,128)(2,1)S(1)} %get-tuple-element.43.refs_0_), channel_id=1, source_target_pairs={{1,2},{3,4},{5,6},{7,0},{2,1},{4,3},{6,5},{0,7},{9,10},{11,12},{13... | collective-permute-start | bytes 589832 | tf_op jit(solution)/shard_map/ppermute | solution.py:469
  5.6 1.4 %collective-permute-start.2 = (bf16[96,1024]{1,0:T(8,128)(2,1)S(1)}, bf16[96,1024]{1,0:T(8,128)(2,1)S(1)}, u32[]{:S(2)}, u32[]{:S(2)}) collective-permute-start(bf16[96,1024]{1,0:T(8,128)(2,1)S(1)} %get-tuple-element.44), channel_id=1, source_target_pairs={{0,8},{8,0},{16,24},{24,16},{32,40},{40,32},{48,56},{56,48},{64,72... | collective-permute-start | bytes 589832 | tf_op jit(solution)/shard_map/ppermute | solution.py:472
  13.8 17.9 %collective-permute-start.11 = (bf16[768,1536]{1,0:T(8,128)(2,1)S(1)}, bf16[768,1536]{1,0:T(8,128)(2,1)S(1)}, u32[]{:S(2)}, u32[]{:S(2)}) collective-permute-start(bf16[768,1536]{1,0:T(8,128)(2,1)S(1)} %pre_grad.1.refs_8_.refs_4_.refs_2_), channel_id=1, source_target_pairs={{0,8},{8,0},{16,24},{24,16},{32,40},{40,32},{48,56},{56,48},{64,72... | collective-permute-start | bytes 7077896 | tf_op jit(solution)/shard_map/ppermute | solution.py:478
  14.4 8.8 %collective-permute-start.6 = (bf16[96,1024]{1,0:T(8,128)(2,1)S(1)}, bf16[96,1024]{1,0:T(8,128)(2,1)S(1)}, u32[]{:S(2)}, u32[]{:S(2)}) collective-permute-start(bf16[96,1024]{1,0:T(8,128)(2,1)S(1)} %collective-permute-done.2.refs_5_), channel_id=1, source_target_pairs={{0,1},{2,3},{4,5},{6,7},{1,0},{3,2},{5,4},{7,6},{8,9},{10,11},{12,... | collective-permute-start | bytes 589832 | tf_op jit(solution)/shard_map/ppermute | solution.py:469
  17.5 7.8 %collective-permute-start.8 = (bf16[96,1024]{1,0:T(8,128)(2,1)S(1)}, bf16[96,1024]{1,0:T(8,128)(2,1)S(1)}, u32[]{:S(2)}, u32[]{:S(2)}) collective-permute-start(bf16[96,1024]{1,0:T(8,128)(2,1)S(1)} %collective-permute-done.2.refs_5_), channel_id=1, source_target_pairs={{1,2},{3,4},{5,6},{7,0},{2,1},{4,3},{6,5},{0,7},{9,10},{11,12},{13... | collective-permute-start | bytes 589832 | tf_op jit(solution)/shard_map/ppermute | solution.py:469
  18.5 11.0 %collective-permute-start.3 = (bf16[96,1024]{1,0:T(8,128)(2,1)S(1)}, bf16[96,1024]{1,0:T(8,128)(2,1)S(1)}, u32[]{:S(2)}, u32[]{:S(2)}) collective-permute-start(bf16[96,1024]{1,0:T(8,128)(2,1)S(1)} %collective-permute-done.refs_1_), channel_id=1, source_target_pairs={{1,2},{3,4},{5,6},{7,0},{2,1},{4,3},{6,5},{0,7},{9,10},{11,12},{13... | collective-permute-start | bytes 589832 | tf_op jit(solution)/shard_map/ppermute | solution.py:469
  19.6 11.1 %collective-permute-start.10 = (bf16[96,1024]{1,0:T(8,128)(2,1)S(1)}, bf16[96,1024]{1,0:T(8,128)(2,1)S(1)}, u32[]{:S(2)}, u32[]{:S(2)}) collective-permute-start(bf16[96,1024]{1,0:T(8,128)(2,1)S(1)} %collective-permute-done.1.refs_2_), channel_id=1, source_target_pairs={{0,1},{2,3},{4,5},{6,7},{1,0},{3,2},{5,4},{7,6},{8,9},{10,11},{12,... | collective-permute-start | bytes 589832 | tf_op jit(solution)/shard_map/ppermute | solution.py:469
  23.2 12.5 %collective-permute-start.7 = (bf16[96,1024]{1,0:T(8,128)(2,1)S(1)}, bf16[96,1024]{1,0:T(8,128)(2,1)S(1)}, u32[]{:S(2)}, u32[]{:S(2)}) collective-permute-start(bf16[96,1024]{1,0:T(8,128)(2,1)S(1)} %collective-permute-done.6.refs_6_), channel_id=1, source_target_pairs={{1,2},{3,4},{5,6},{7,0},{2,1},{4,3},{6,5},{0,7},{9,10},{11,12},{13... | collective-permute-start | bytes 589832 | tf_op jit(solution)/shard_map/ppermute | solution.py:469
  25.3 10.4 %collective-permute-start.9 = (bf16[96,1024]{1,0:T(8,128)(2,1)S(1)}, bf16[96,1024]{1,0:T(8,128)(2,1)S(1)}, u32[]{:S(2)}, u32[]{:S(2)}) collective-permute-start(bf16[96,1024]{1,0:T(8,128)(2,1)S(1)} %collective-permute-done.8.refs_7_), channel_id=1, source_target_pairs={{0,1},{2,3},{4,5},{6,7},{1,0},{3,2},{5,4},{7,6},{8,9},{10,11},{12,... | collective-permute-start | bytes 589832 | tf_op jit(solution)/shard_map/ppermute | solution.py:469
  29.5 8.3 %collective-permute-start.4 = (bf16[96,1024]{1,0:T(8,128)(2,1)S(1)}, bf16[96,1024]{1,0:T(8,128)(2,1)S(1)}, u32[]{:S(2)}, u32[]{:S(2)}) collective-permute-start(bf16[96,1024]{1,0:T(8,128)(2,1)S(1)} %collective-permute-done.3.refs_3_), channel_id=1, source_target_pairs={{0,1},{2,3},{4,5},{6,7},{1,0},{3,2},{5,4},{7,6},{8,9},{10,11},{12,... | collective-permute-start | bytes 589832 | tf_op jit(solution)/shard_map/ppermute | solution.py:469
  30.7 8.2 %collective-permute-start.14 = (bf16[96,1024]{1,0:T(8,128)(2,1)S(1)}, bf16[96,1024]{1,0:T(8,128)(2,1)S(1)}, u32[]{:S(2)}, u32[]{:S(2)}) collective-permute-start(bf16[96,1024]{1,0:T(8,128)(2,1)S(1)} %collective-permute-done.10.refs_4_), channel_id=1, source_target_pairs={{1,2},{3,4},{5,6},{7,0},{2,1},{4,3},{6,5},{0,7},{9,10},{11,12},{13... | collective-permute-start | bytes 589832 | tf_op jit(solution)/shard_map/ppermute | solution.py:469
  35.7 7.0 %collective-permute-start.12 = (bf16[96,1024]{1,0:T(8,128)(2,1)S(1)}, bf16[96,1024]{1,0:T(8,128)(2,1)S(1)}, u32[]{:S(2)}, u32[]{:S(2)}) collective-permute-start(bf16[96,1024]{1,0:T(8,128)(2,1)S(1)} %collective-permute-done.7.refs_2_), channel_id=1, source_target_pairs={{0,1},{2,3},{4,5},{6,7},{1,0},{3,2},{5,4},{7,6},{8,9},{10,11},{12,... | collective-permute-start | bytes 589832 | tf_op jit(solution)/shard_map/ppermute | solution.py:469
  36.9 6.3 %collective-permute-start.13 = (bf16[96,1024]{1,0:T(8,128)(2,1)S(1)}, bf16[96,1024]{1,0:T(8,128)(2,1)S(1)}, u32[]{:S(2)}, u32[]{:S(2)}) collective-permute-start(bf16[96,1024]{1,0:T(8,128)(2,1)S(1)} %collective-permute-done.9.refs_3_), channel_id=1, source_target_pairs={{1,2},{3,4},{5,6},{7,0},{2,1},{4,3},{6,5},{0,7},{9,10},{11,12},{13... | collective-permute-start | bytes 589832 | tf_op jit(solution)/shard_map/ppermute | solution.py:469
  37.9 12.9 %collective-permute-start.5 = (bf16[96,1024]{1,0:T(8,128)(2,1)S(1)}, bf16[96,1024]{1,0:T(8,128)(2,1)S(1)}, u32[]{:S(2)}, u32[]{:S(2)}) collective-permute-start(bf16[96,1024]{1,0:T(8,128)(2,1)S(1)} %collective-permute-done.4.refs_0_), channel_id=1, source_target_pairs={{1,2},{3,4},{5,6},{7,0},{2,1},{4,3},{6,5},{0,7},{9,10},{11,12},{13... | collective-permute-start | bytes 589832 | tf_op jit(solution)/shard_map/ppermute | solution.py:486
  43.1 7.7 %collective-permute-start.15 = (bf16[96,1024]{1,0:T(8,128)(2,1)S(1)}, bf16[96,1024]{1,0:T(8,128)(2,1)S(1)}, u32[]{:S(2)}, u32[]{:S(2)}) collective-permute-start(bf16[96,1024]{1,0:T(8,128)(2,1)S(1)} %collective-permute-done.13.refs_1_), channel_id=1, source_target_pairs={{0,1},{2,3},{4,5},{6,7},{1,0},{3,2},{5,4},{7,6},{8,9},{10,11},{12,... | collective-permute-start | bytes 589832 | tf_op jit(solution)/shard_map/ppermute | solution.py:489
  52.6 11.4 %collective-permute-start.22 = (bf16[128,1536]{1,0:T(8,128)(2,1)S(1)}, bf16[128,1536]{1,0:T(8,128)(2,1)S(1)}, u32[]{:S(2)}, u32[]{:S(2)}) collective-permute-start(bf16[128,1536]{1,0:T(8,128)(2,1)S(1)} %get-tuple-element.65), channel_id=1, source_target_pairs={{0,64},{8,72},{16,80},{24,88},{32,96},{40,104},{48,112},{56,120},{... | collective-permute-start | bytes 1179656 | tf_op jit(solution)/shard_map/ppermute | solution.py:496
  54.3 16.6 %collective-permute-start.23 = (bf16[128,1536]{1,0:T(8,128)(2,1)S(1)}, bf16[128,1536]{1,0:T(8,128)(2,1)S(1)}, u32[]{:S(2)}, u32[]{:S(2)}) collective-permute-start(bf16[128,1536]{1,0:T(8,128)(2,1)S(1)} %get-tuple-element.66), channel_id=1, source_target_pairs={{0,192},{8,200},{16,208},{24,216},{32,224},{40,232},{48,240},{56,2... | collective-permute-start | bytes 1179656 | tf_op jit(solution)/shard_map/ppermute | solution.py:496
  56.5 14.4 %collective-permute-start.24 = (bf16[128,1536]{1,0:T(8,128)(2,1)S(1)}, bf16[128,1536]{1,0:T(8,128)(2,1)S(1)}, u32[]{:S(2)}, u32[]{:S(2)}) collective-permute-start(bf16[128,1536]{1,0:T(8,128)(2,1)S(1)} %get-tuple-element.67), channel_id=1, source_target_pairs={{0,128},{8,136},{16,144},{24,152},{32,160},{40,168},{48,176},{56,1... | collective-permute-start | bytes 1179656 | tf_op jit(solution)/shard_map/ppermute | solution.py:496
  59.0 16.5 %collective-permute-start.16 = (bf16[128,1536]{1,0:T(8,128)(2,1)S(1)}, bf16[128,1536]{1,0:T(8,128)(2,1)S(1)}, u32[]{:S(2)}, u32[]{:S(2)}) collective-permute-start(bf16[128,1536]{1,0:T(8,128)(2,1)S(1)} %get-tuple-element.57), channel_id=1, source_target_pairs={{0,16},{8,24},{16,0},{24,8},{32,48},{40,56},{48,32},{56,40},{64,80... | collective-permute-start | bytes 1179656 | tf_op jit(solution)/shard_map/ppermute | solution.py:496
  60.6 16.2 %collective-permute-start.17 = (bf16[128,1536]{1,0:T(8,128)(2,1)S(1)}, bf16[128,1536]{1,0:T(8,128)(2,1)S(1)}, u32[]{:S(2)}, u32[]{:S(2)}) collective-permute-start(bf16[128,1536]{1,0:T(8,128)(2,1)S(1)} %get-tuple-element.58), channel_id=1, source_target_pairs={{0,48},{8,56},{16,32},{24,40},{32,16},{40,24},{48,0},{56,8},{64,11... | collective-permute-start | bytes 1179656 | tf_op jit(solution)/shard_map/ppermute | solution.py:496
  64.0 14.5 %collective-permute-start.18 = (bf16[128,1536]{1,0:T(8,128)(2,1)S(1)}, bf16[128,1536]{1,0:T(8,128)(2,1)S(1)}, u32[]{:S(2)}, u32[]{:S(2)}) collective-permute-start(bf16[128,1536]{1,0:T(8,128)(2,1)S(1)} %get-tuple-element.59), channel_id=1, source_target_pairs={{0,32},{8,40},{16,48},{24,56},{32,0},{40,8},{48,16},{56,24},{64,96... | collective-permute-start | bytes 1179656 | tf_op jit(solution)/shard_map/ppermute | solution.py:496
  71.9 10.9 %collective-permute-start.25 = (bf16[32,1536]{1,0:T(8,128)(2,1)S(1)}, bf16[32,1536]{1,0:T(8,128)(2,1)S(1)}, u32[]{:S(2)}, u32[]{:S(2)}) collective-permute-start(bf16[32,1536]{1,0:T(8,128)(2,1)S(1)} %get-tuple-element.69), channel_id=1, source_target_pairs={{0,16},{8,24},{16,0},{24,8},{32,48},{40,56},{48,32},{56,40},{64,80... | collective-permute-start | bytes 294920 | tf_op jit(solution)/shard_map/ppermute | solution.py:499
  73.4 10.3 %collective-permute-start.26 = (bf16[32,1536]{1,0:T(8,128)(2,1)S(1)}, bf16[32,1536]{1,0:T(8,128)(2,1)S(1)}, u32[]{:S(2)}, u32[]{:S(2)}) collective-permute-start(bf16[32,1536]{1,0:T(8,128)(2,1)S(1)} %get-tuple-element.70), channel_id=1, source_target_pairs={{0,48},{8,56},{16,32},{24,40},{32,16},{40,24},{48,0},{56,8},{64,11... | collective-permute-start | bytes 294920 | tf_op jit(solution)/shard_map/ppermute | solution.py:499
  75.5 8.2 %collective-permute-start.27 = (bf16[32,1536]{1,0:T(8,128)(2,1)S(1)}, bf16[32,1536]{1,0:T(8,128)(2,1)S(1)}, u32[]{:S(2)}, u32[]{:S(2)}) collective-permute-start(bf16[32,1536]{1,0:T(8,128)(2,1)S(1)} %get-tuple-element.71), channel_id=1, source_target_pairs={{0,32},{8,40},{16,48},{24,56},{32,0},{40,8},{48,16},{56,24},{64,96... | collective-permute-start | bytes 294920 | tf_op jit(solution)/shard_map/ppermute | solution.py:499
  79.5 4.7 %collective-permute-start.19 = (bf16[32,1536]{1,0:T(8,128)(2,1)S(1)}, bf16[32,1536]{1,0:T(8,128)(2,1)S(1)}, u32[]{:S(2)}, u32[]{:S(2)}) collective-permute-start(bf16[32,1536]{1,0:T(8,128)(2,1)S(1)} %get-tuple-element.61), channel_id=1, source_target_pairs={{0,64},{8,72},{16,80},{24,88},{32,96},{40,104},{48,112},{56,120},{... | collective-permute-start | bytes 294920 | tf_op jit(solution)/shard_map/ppermute | solution.py:499
  80.6 5.8 %collective-permute-start.20 = (bf16[32,1536]{1,0:T(8,128)(2,1)S(1)}, bf16[32,1536]{1,0:T(8,128)(2,1)S(1)}, u32[]{:S(2)}, u32[]{:S(2)}) collective-permute-start(bf16[32,1536]{1,0:T(8,128)(2,1)S(1)} %get-tuple-element.62), channel_id=1, source_target_pairs={{0,192},{8,200},{16,208},{24,216},{32,224},{40,232},{48,240},{56,2... | collective-permute-start | bytes 294920 | tf_op jit(solution)/shard_map/ppermute | solution.py:499
  82.8 6.1 %collective-permute-start.21 = (bf16[32,1536]{1,0:T(8,128)(2,1)S(1)}, bf16[32,1536]{1,0:T(8,128)(2,1)S(1)}, u32[]{:S(2)}, u32[]{:S(2)}) collective-permute-start(bf16[32,1536]{1,0:T(8,128)(2,1)S(1)} %get-tuple-element.63), channel_id=1, source_target_pairs={{0,128},{8,136},{16,144},{24,152},{32,160},{40,168},{48,176},{56,1... | collective-permute-start | bytes 294920 | tf_op jit(solution)/shard_map/ppermute | solution.py:499
  90.4 16.0 %all-to-all-start = ((bf16[32,16,512]{2,1,0:T(8,128)(2,1)}), bf16[32,16,512]{2,1,0:T(8,128)(2,1)S(1)}, u32[]{:S(2)}, u32[]{:S(2)}) async-start(bf16[32,16,512]{2,1,0:T(8,128)(2,1)} %second_sum.1), calls=%async_computation | async-start | bytes 1048576 | tf_op jit(solution)/shard_map/all_to_all | solution.py:501
  125.7 6.9 %collective-permute-start.28 = (bf16[16,1536]{1,0:T(8,128)(2,1)S(1)}, bf16[16,1536]{1,0:T(8,128)(2,1)S(1)}, u32[]{:S(2)}, u32[]{:S(2)}) collective-permute-start(bf16[16,1536]{1,0:T(8,128)(2,1)S(1)} %get-tuple-element.74), channel_id=1, source_target_pairs={{0,64},{8,72},{16,80},{24,88},{32,96},{40,104},{48,112},{56,120},{... | collective-permute-start | bytes 147464 | tf_op jit(solution)/shard_map/ppermute | solution.py:509
  125.8 6.8 %collective-permute-start.29 = (bf16[16,1536]{1,0:T(8,128)(2,1)S(1)}, bf16[16,1536]{1,0:T(8,128)(2,1)S(1)}, u32[]{:S(2)}, u32[]{:S(2)}) collective-permute-start(bf16[16,1536]{1,0:T(8,128)(2,1)S(1)} %get-tuple-element.75), channel_id=1, source_target_pairs={{0,128},{8,136},{16,144},{24,152},{32,160},{40,168},{48,176},{56,1... | collective-permute-start | bytes 147464 | tf_op jit(solution)/shard_map/ppermute | solution.py:509
  128.0 5.3 %collective-permute-start.30 = (bf16[16,1536]{1,0:T(8,128)(2,1)S(1)}, bf16[16,1536]{1,0:T(8,128)(2,1)S(1)}, u32[]{:S(2)}, u32[]{:S(2)}) collective-permute-start(bf16[16,1536]{1,0:T(8,128)(2,1)S(1)} %get-tuple-element.76), channel_id=1, source_target_pairs={{0,192},{8,200},{16,208},{24,216},{32,224},{40,232},{48,240},{56,2... | collective-permute-start | bytes 147464 | tf_op jit(solution)/shard_map/ppermute | solution.py:509
  (14 other events, 233.0 us)
